TPU v7x, 512 devices: a whole 4x4x16 slice. The times are simulated.
512 devices in a mesh: ens: 8 (over z_lo), lat: 4 (over z_hi, core), lon: 16 (over x, y).
Axes of the slice: x: 4, y: 4, z: 16 (z_hi: 2, z_lo: 8; z = z_hi * 8 + z_lo), core: 2. Of those that a mesh axis runs over, the one named last changes fastest.
Arguments:
- grad_tokens: bfloat16 [104, 131072], P(None, ('lat', 'lon')), may hold values from -6 to 6
- token_index: int32 [64, 2048], P('lat', 'lon'), may hold values from 0 to 131071, as said below
- members: bfloat16 [16, 104, 64, 2048], P('ens', None, 'lat', 'lon'), may hold values from -6 to 6
- lat_taps: float32 [17], replicated, may hold values from 0.05 to 1
- lon_taps: float32 [17], replicated, may hold values from 0.05 to 1
Outputs:
- increment: float32 [104, 64, 2048], P('ens', 'lat', 'lon')
Inputs may be any that keep to these rules, and one draw needn't show every extreme that they name: `token_index`: every token is the token of exactly one cell. With grid blocks numbered b = (latitude block) * (longitude blocks) + (longitude block), each of 16 x 128 cells, the cells of block b that take tokens from s * 2048 .. (s + 1) * 2048 - 1 take exactly the tokens s * 2048 + b * 32 + k for k = 0 .. 31, in any order over the block's cells.
All inputs are finite; a program needn't handle non-finite values.
Results may differ from a plain program's by a relative error of at most 0.0003.
Values may be sent and summed in bfloat16 or wider, within the bound.
A program may use at most 64 MiB of HBM per device.

v0:
```python
import jax
import jax.numpy as jnp
from jax import lax
from jax.sharding import PartitionSpec as P


def with_halo(shard, sides, width):
    for axis, dim in sides:
        size, length = (lax.axis_size(axis), shard.shape[dim])
        up = [(i, (i + 1) % size) for i in range(size)]
        down = [(j, i) for i, j in up]
        last = lax.slice_in_dim(shard, length - width, length, axis=dim)
        first = lax.slice_in_dim(shard, 0, width, axis=dim)
        before = lax.ppermute(last, axis, up)
        after = lax.ppermute(first, axis, down)
        shard = jnp.concatenate([before, shard, after], axis=dim)
    return shard


def split_up(shard, dim, size):
    before, after = (shard.shape[:dim], shard.shape[dim + 1 :])
    return jnp.moveaxis(shard.reshape(*before, size, -1, *after), dim, 0)


def sent_and_summed(shard, axis, dim):
    size = lax.axis_size(axis)
    pieces = lax.all_to_all(split_up(shard, dim, size), axis, 0, 0, tiled=True)
    return jnp.sum(pieces, axis=0)


def banded(taps, length, radius):
    upper = jnp.arange(length + 2 * radius, dtype=jnp.int32)[:, None]
    lower = jnp.arange(length, dtype=jnp.int32)[None, :]
    offset = upper - lower
    picks = (
        offset[:, :, None] == jnp.arange(2 * radius + 1, dtype=jnp.int32)[None, None, :]
    ).astype(jnp.float32)
    return jnp.einsum("uiq,q->ui", picks, taps, precision=lax.Precision.HIGHEST)


def edge_keep(rows, radius):
    lat_pos = lax.axis_index("lat")
    lat_count = lax.axis_size("lat")
    row_ids = jnp.arange(rows, dtype=jnp.int32)
    keep_top = jnp.where(lat_pos > 0, 1.0, 0.0)
    keep_bottom = jnp.where(lat_pos < lat_count - 1, 1.0, 0.0)
    keep = jnp.where(
        row_ids < radius, keep_top, jnp.where(row_ids >= rows - radius, keep_bottom, 1.0)
    )
    return keep.astype(jnp.float32)


def localize(field, lat_w, lon_w):
    radius = (lat_w.shape[0] - 1) // 2
    lat_rows = field.shape[2]
    lon_cols = field.shape[3]
    lat_matrix = banded(lat_w, lat_rows, radius)
    lon_matrix = banded(lon_w, lon_cols, radius)
    padded = with_halo(field, (("lat", 2),), radius)
    padded = padded * edge_keep(padded.shape[2], radius)[:, None]
    middle = jnp.einsum("mcul,ui->mcil", padded, lat_matrix, precision=lax.Precision.HIGHEST)
    widened = with_halo(middle, (("lon", 3),), radius)
    return jnp.einsum("mciu,uj->mcij", widened, lon_matrix, precision=lax.Precision.HIGHEST)


def local(grad_tokens, token_index, members, lat_taps, lon_taps):
    channels, cells = grad_tokens.shape
    lat_rows, lon_cols = token_index.shape
    lon_count = lax.axis_size("lon")
    blocks = lax.axis_size("lat") * lon_count
    piece = cells // blocks
    block_id = lax.axis_index("lat") * lon_count + lax.axis_index("lon")
    wanted = token_index.reshape(-1)
    source = wanted // cells
    offset = source * piece + wanted % cells - block_id * piece
    moved = lax.all_to_all(
        grad_tokens.reshape(channels, blocks, piece),
        ("lat", "lon"),
        split_axis=1,
        concat_axis=1,
        tiled=True,
    )
    grid = jnp.take(moved.reshape(channels, cells), offset, axis=1)
    grid_plain = grid.reshape(channels, lat_rows, lon_cols)
    weighted = members.astype(jnp.float32) * grid_plain.astype(jnp.float32)[None]
    control = localize(weighted, lat_taps[::-1], lon_taps[::-1])
    smoothed = localize(control, lat_taps, lon_taps)
    partial_total = jnp.sum(members.astype(jnp.float32) * smoothed, axis=0)
    summed = sent_and_summed(partial_total, "ens", 0)
    return summed / (lax.axis_size("ens") * members.shape[0] - 1)


def solution(mesh):
    in_specs = (P(None, ("lat", "lon")), P("lat", "lon"), P("ens", None, "lat", "lon"), P(), P())
    out_specs = P("ens", "lat", "lon")
    return jax.shard_map(local, mesh=mesh, in_specs=in_specs, out_specs=out_specs, check_vma=False)
```

profile of v0, /device:TPU:1, one launch (start us, length us, event | category | flops | bytes accessed | tf_op | source)
XLA Modules:
  0.0 299.6 jit_solution(5869311120649960038)
XLA Ops:
  0.0 2.0 copy.20
  2.0 22.2 %all-to-all-start = ((bf16[104,64,32]{0,2,1:T(8,128)(2,1)}), bf16[104,64,32]{0,2,1:T(8,128)(2,1)S(1)}, u32[]{:S(2)}, u32[]{:S(2)}) async-start(bf16[104,64,32]{0,2,1:T(8,128)(2,1)} %bitcast.8), calls=%async_computation | async-start | bytes 1048576 | tf_op jit(solution)/shard_map/all_to_all | solution.py:76
  24.3 0.0 copy-done.5
  24.3 0.1 compare_select_fusion
  24.4 20.5 %all-to-all-done = bf16[104,64,32]{0,2,1:T(8,128)(2,1)S(1)} async-done(((bf16[104,64,32]{0,2,1:T(8,128)(2,1)}), bf16[104,64,32]{0,2,1:T(8,128)(2,1)S(1)}, u32[]{:S(2)}, u32[]{:S(2)}) %all-to-all-start) | async-done | bytes 426016 | tf_op jit(solution)/shard_map/all_to_all | solution.py:76
  45.0 6.2 %gather_fusion = bf16[2048,104]{1,0:T(8,128)(2,1)S(1)} fusion(bf16[104,2048]{0,1:T(8,128)(2,1)S(1)} %bitcast.52, s32[2048]{0:T(1024)S(1)} %broadcast_clamp_fusion), kind=kCustom, calls=%fused_computation | custom fusion | bytes 860160 | tf_op jit(solution)/shard_map/jit(_take)/gather | solution.py:83
  51.1 0.0 copy-start
  51.2 0.4 copy.21
  51.5 0.1 select_convert_fusion
  51.6 0.7 copy-done
  52.3 0.1 convert_multiply_fusion.1
  52.4 0.0 copy-start.8
  52.5 0.0 copy-start.10
  52.5 1.3 fusion.56
  53.8 3.1 %collective-permute-start = (f32[2,104,8,128]{3,2,1,0:T(8,128)}, f32[2,104,8,128]{3,2,1,0:T(8,128)S(1)}, u32[]{:S(2)}, u32[]{:S(2)}) collective-permute-start(f32[2,104,8,128]{3,2,1,0:T(8,128)} %get-tuple-element.11), channel_id=1, source_target_pairs={{0,16},{16,32},{32,48},{48,0},{1,17},{17,33},{33,49},{49,1},{2,18}... | collective-permute-start | bytes 2555912 | tf_op jit(solution)/shard_map/ppermute | solution.py:14
  56.9 2.1 collective-permute-start.1
  58.9 0.0 copy-done.8
  59.0 0.1 rev.6
  59.1 0.0 copy-done.10
  59.1 0.6 rev.7
  59.7 1.1 fusion.33
  60.8 0.9 iota_compare_fusion
  61.7 5.1 %collective-permute-done = f32[2,104,8,128]{3,2,1,0:T(8,128)S(1)} collective-permute-done((f32[2,104,8,128]{3,2,1,0:T(8,128)}, f32[2,104,8,128]{3,2,1,0:T(8,128)S(1)}, u32[]{:S(2)}, u32[]{:S(2)}) %collective-permute-start) | collective-permute-done | bytes 852000 | tf_op jit(solution)/shard_map/ppermute | solution.py:14
  66.8 74.9 %collective-permute-done.1 = f32[2,104,8,128]{3,2,1,0:T(8,128)S(1)} collective-permute-done((f32[2,104,8,128]{3,2,1,0:T(8,128)}, f32[2,104,8,128]{3,2,1,0:T(8,128)S(1)}, u32[]{:S(2)}, u32[]{:S(2)}) %collective-permute-start.1) | collective-permute-done | bytes 852000 | tf_op jit(solution)/shard_map/ppermute | solution.py:15
  141.7 0.9 copy-done.2
  142.6 3.3 %fusion.32 = f32[2,104,16,128]{3,2,1,0:T(8,128)S(1)} fusion(f32[32,16,1,1]{1,0,3,2:T(8,128)S(1)} %bitcast.59, f32[2,104,8,128]{3,2,1,0:T(8,128)} %copy-done.2, f32[2,104,16,128]{3,2,1,0:T(8,128)S(1)} %convert_multiply_fusion.1, f32[2,104,8,128]{3,2,1,0:T(8,128)} %copy-done.1, f32[32]{0:T(128)S(1)} %compare_select_fusion.6), kind=kOutput, calls=%fused_computation.35 | convolution fusion | flops 166133760 | bytes 5113984 | tf_op jit(solution)/shard_map/mcul,ui->mcil/dot_general | solution.py:61
  145.9 1.8 fusion.55
  147.7 2.7 copy.22
  150.4 0.6 copy.23
  151.0 1.9 collective-permute-start.3
  152.9 3.5 %collective-permute-start.2 = (f32[2,104,16,8]{1,3,2,0:T(8,128)}, f32[2,104,16,8]{1,3,2,0:T(8,128)}, u32[]{:S(2)}, u32[]{:S(2)}) collective-permute-start(f32[2,104,16,8]{1,3,2,0:T(8,128)} %copy.22), channel_id=1, source_target_pairs={{0,1},{1,2},{2,3},{3,4},{4,5},{5,6},{6,7},{7,8},{8,9},{9,10},{10,1... | collective-permute-start | bytes 319496 | tf_op jit(solution)/shard_map/ppermute | solution.py:14
  156.5 2.2 fusion.27
  158.7 3.5 %collective-permute-done.2 = f32[2,104,16,8]{1,3,2,0:T(8,128)} collective-permute-done((f32[2,104,16,8]{1,3,2,0:T(8,128)}, f32[2,104,16,8]{1,3,2,0:T(8,128)}, u32[]{:S(2)}, u32[]{:S(2)}) %collective-permute-start.2) | collective-permute-done | bytes 106528 | tf_op jit(solution)/shard_map/ppermute | solution.py:14
  162.3 1.6 copy.24
  163.9 0.0 collective-permute-done.3
  163.9 0.0 copy-start.3
  164.0 2.8 copy.25
  166.7 0.0 copy-done.3
  166.7 4.8 %fusion.5 = f32[2,104,16,128]{3,2,1,0:T(8,128)S(1)} fusion(f32[144,128,1,1]{1,0,3,2:T(8,128)S(1)} %bitcast.55, f32[2,104,16,8]{3,2,1,0:T(8,128)} %copy.25, f32[2,104,16,128]{3,2,1,0:T(8,128)S(1)} %fusion.32, f32[2,104,16,8]{3,2,1,0:T(8,128)S(1)} %copy.24), kind=kOutput, calls=%fused_computation.7 | convolution fusion | flops 737058816 | bytes 3694592 | tf_op jit(solution)/shard_map/mciu,uj->mcij/dot_general | solution.py:63
  171.5 0.0 copy-start.9
  171.5 0.1 fusion.54
  171.7 1.9 collective-permute-start.4
  173.6 2.4 collective-permute-start.5
  176.0 0.0 copy-done.9
  176.0 1.1 fusion.34
  177.1 46.9 %collective-permute-done.4 = f32[2,104,8,128]{3,2,1,0:T(8,128)S(1)} collective-permute-done((f32[2,104,8,128]{3,2,1,0:T(8,128)S(1)}, f32[2,104,8,128]{3,2,1,0:T(8,128)S(1)}, u32[]{:S(2)}, u32[]{:S(2)}) %collective-permute-start.4) | collective-permute-done | bytes 852000 | tf_op jit(solution)/shard_map/ppermute | solution.py:14
  224.0 0.0 collective-permute-done.5
  224.0 1.9 fusion.31
  225.9 1.8 fusion.53
  227.7 2.7 copy.26
  230.4 0.6 copy.27
  231.0 1.9 collective-permute-start.7
  233.0 3.6 %collective-permute-start.6 = (f32[2,104,16,8]{1,3,2,0:T(8,128)}, f32[2,104,16,8]{1,3,2,0:T(8,128)}, u32[]{:S(2)}, u32[]{:S(2)}) collective-permute-start(f32[2,104,16,8]{1,3,2,0:T(8,128)} %copy.26), channel_id=1, source_target_pairs={{0,1},{1,2},{2,3},{3,4},{4,5},{5,6},{6,7},{7,8},{8,9},{9,10},{10,1... | collective-permute-start | bytes 319496 | tf_op jit(solution)/shard_map/ppermute | solution.py:14
  236.6 2.2 fusion.25
  238.8 4.3 %collective-permute-done.6 = f32[2,104,16,8]{1,3,2,0:T(8,128)} collective-permute-done((f32[2,104,16,8]{1,3,2,0:T(8,128)}, f32[2,104,16,8]{1,3,2,0:T(8,128)}, u32[]{:S(2)}, u32[]{:S(2)}) %collective-permute-start.6) | collective-permute-done | bytes 106528 | tf_op jit(solution)/shard_map/ppermute | solution.py:14
  243.1 1.6 copy.28
  244.7 0.0 collective-permute-done.7
  244.7 0.0 copy-start.4
  244.8 2.8 copy.29
  247.5 0.0 copy-done.4
  247.5 5.0 %fusion.22 = f32[104,16,128]{2,1,0:T(8,128)S(1)} fusion(bf16[2,104,16,128]{3,2,1,0:T(8,128)(2,1)} %param.7, f32[144,128,1,1]{1,0,3,2:T(8,128)S(1)} %bitcast.56, f32[2,104,16,8]{3,2,1,0:T(8,128)} %copy.29, f32[2,104,16,128]{3,2,1,0:T(8,128)S(1)} %fusion.31, f32[2,104,16,8]{3,2,1,0:T(8,128)S(1)} %copy.28), kind=kOutput, calls=%fused_computation.27 | convolution fusion | flops 738123776 | bytes 3694592 | tf_op jit(solution)/shard_map/mciu,uj->mcij/dot_general | solution.py:63
  252.5 46.3 %all_to_all.10 = f32[8,13,16,128]{3,2,1,0:T(8,128)S(1)} all-to-all(f32[8,13,16,128]{3,2,1,0:T(8,128)S(1)} %bitcast.53), channel_id=1, replica_groups=mesh['ens'=8,'lat'=4,'lon'=16] {'ens'}, dimensions={0} | all-to-all | bytes 1703936 | tf_op jit(solution)/shard_map/all_to_all | solution.py:27
  298.9 0.1 reduce_sum.19
  298.9 0.7 broadcast_multiply_fusion
  (15 shorter events, 0.1 us)
Async XLA Ops:
  0.0 24.3 %copy-start.5 = (s32[16,128]{1,0:T(8,128)S(1)}, s32[16,128]{1,0:T(8,128)}, u32[]{:S(2)}) copy-start(s32[16,128]{1,0:T(8,128)} %param.6) | copy-start | bytes 24580
  2.0 42.9 %all-to-all-start = ((bf16[104,64,32]{0,2,1:T(8,128)(2,1)}), bf16[104,64,32]{0,2,1:T(8,128)(2,1)S(1)}, u32[]{:S(2)}, u32[]{:S(2)}) async-start(bf16[104,64,32]{0,2,1:T(8,128)(2,1)} %bitcast.8), calls=%async_computation | async-start | bytes 1048576 | tf_op jit(solution)/shard_map/all_to_all | solution.py:76
  51.1 1.2 copy-start
  52.4 6.5 %copy-start.8 = (f32[17]{0:T(128)S(1)}, f32[17]{0:T(128)}, u32[]{:S(2)}) copy-start(f32[17]{0:T(128)} %param.8) | copy-start | bytes 208
  52.5 6.6 %copy-start.10 = (f32[17]{0:T(128)S(1)}, f32[17]{0:T(128)}, u32[]{:S(2)}) copy-start(f32[17]{0:T(128)} %param.9) | copy-start | bytes 208
  53.8 13.0 %collective-permute-start = (f32[2,104,8,128]{3,2,1,0:T(8,128)}, f32[2,104,8,128]{3,2,1,0:T(8,128)S(1)}, u32[]{:S(2)}, u32[]{:S(2)}) collective-permute-start(f32[2,104,8,128]{3,2,1,0:T(8,128)} %get-tuple-element.11), channel_id=1, source_target_pairs={{0,16},{16,32},{32,48},{48,0},{1,17},{17,33},{33,49},{49,1},{2,18}... | collective-permute-start | bytes 2555912 | tf_op jit(solution)/shard_map/ppermute | solution.py:14
  56.9 84.8 %collective-permute-start.1 = (f32[2,104,8,128]{3,2,1,0:T(8,128)}, f32[2,104,8,128]{3,2,1,0:T(8,128)S(1)}, u32[]{:S(2)}, u32[]{:S(2)}) collective-permute-start(f32[2,104,8,128]{3,2,1,0:T(8,128)} %get-tuple-element.12), channel_id=1, source_target_pairs={{16,0},{32,16},{48,32},{0,48},{17,1},{33,17},{49,33},{1,49},{18,2}... | collective-permute-start | bytes 2555912 | tf_op jit(solution)/shard_map/ppermute | solution.py:15
  59.7 86.2 %copy-start.6 = (f32[32]{0:T(128)}, f32[32]{0:T(128)S(1)}, u32[]{:S(2)}) copy-start(f32[32]{0:T(128)S(1)} %compare_select_fusion.6) | copy-start | bytes 388
  66.8 74.9 %copy-start.1 = (f32[2,104,8,128]{3,2,1,0:T(8,128)}, f32[2,104,8,128]{3,2,1,0:T(8,128)S(1)}, u32[]{:S(2)}) copy-start(f32[2,104,8,128]{3,2,1,0:T(8,128)S(1)} %collective-permute-done) | copy-start | bytes 2555908
  141.7 0.9 copy-start.2
  151.0 12.9 %collective-permute-start.3 = (f32[2,104,16,8]{1,3,2,0:T(8,128)S(1)}, f32[2,104,16,8]{1,3,2,0:T(8,128)}, u32[]{:S(2)}, u32[]{:S(2)}) collective-permute-start(f32[2,104,16,8]{1,3,2,0:T(8,128)S(1)} %copy.23), channel_id=1, source_target_pairs={{1,0},{2,1},{3,2},{4,3},{5,4},{6,5},{7,6},{8,7},{9,8},{10,9},{11,1... | collective-permute-start | bytes 319496 | tf_op jit(solution)/shard_map/ppermute | solution.py:15
  152.9 9.3 %collective-permute-start.2 = (f32[2,104,16,8]{1,3,2,0:T(8,128)}, f32[2,104,16,8]{1,3,2,0:T(8,128)}, u32[]{:S(2)}, u32[]{:S(2)}) collective-permute-start(f32[2,104,16,8]{1,3,2,0:T(8,128)} %copy.22), channel_id=1, source_target_pairs={{0,1},{1,2},{2,3},{3,4},{4,5},{5,6},{6,7},{7,8},{8,9},{9,10},{10,1... | collective-permute-start | bytes 319496 | tf_op jit(solution)/shard_map/ppermute | solution.py:14
  163.9 2.8 copy-start.3
  171.5 4.5 %copy-start.9 = (f32[17]{0:T(128)S(1)}, f32[17]{0:T(128)}, u32[]{:S(2)}) copy-start(f32[17]{0:T(128)} %param.8) | copy-start | bytes 208
  171.5 52.5 %copy-start.7 = (f32[32]{0:T(128)S(1)}, f32[32]{0:T(128)}, u32[]{:S(2)}) copy-start(f32[32]{0:T(128)} %copy-done.6) | copy-start | bytes 388
  171.7 52.3 %collective-permute-start.4 = (f32[2,104,8,128]{3,2,1,0:T(8,128)S(1)}, f32[2,104,8,128]{3,2,1,0:T(8,128)S(1)}, u32[]{:S(2)}, u32[]{:S(2)}) collective-permute-start(f32[2,104,8,128]{3,2,1,0:T(8,128)S(1)} %get-tuple-element.7), channel_id=1, source_target_pairs={{0,16},{16,32},{32,48},{48,0},{1,17},{17,33},{33,49},{49,1},{2,18}... | collective-permute-start | bytes 2555912 | tf_op jit(solution)/shard_map/ppermute | solution.py:14
  173.6 50.4 %collective-permute-start.5 = (f32[2,104,8,128]{3,2,1,0:T(8,128)S(1)}, f32[2,104,8,128]{3,2,1,0:T(8,128)S(1)}, u32[]{:S(2)}, u32[]{:S(2)}) collective-permute-start(f32[2,104,8,128]{3,2,1,0:T(8,128)S(1)} %get-tuple-element.8), channel_id=1, source_target_pairs={{16,0},{32,16},{48,32},{0,48},{17,1},{33,17},{49,33},{1,49},{18,2}... | collective-permute-start | bytes 2555912 | tf_op jit(solution)/shard_map/ppermute | solution.py:15
  227.7 8.9 %copy-start.11 = (f32[17]{0:T(128)S(1)}, f32[17]{0:T(128)}, u32[]{:S(2)}) copy-start(f32[17]{0:T(128)} %param.9) | copy-start | bytes 208
  231.0 13.7 %collective-permute-start.7 = (f32[2,104,16,8]{1,3,2,0:T(8,128)S(1)}, f32[2,104,16,8]{1,3,2,0:T(8,128)}, u32[]{:S(2)}, u32[]{:S(2)}) collective-permute-start(f32[2,104,16,8]{1,3,2,0:T(8,128)S(1)} %copy.27), channel_id=1, source_target_pairs={{1,0},{2,1},{3,2},{4,3},{5,4},{6,5},{7,6},{8,7},{9,8},{10,9},{11,1... | collective-permute-start | bytes 319496 | tf_op jit(solution)/shard_map/ppermute | solution.py:15
  233.0 10.1 %collective-permute-start.6 = (f32[2,104,16,8]{1,3,2,0:T(8,128)}, f32[2,104,16,8]{1,3,2,0:T(8,128)}, u32[]{:S(2)}, u32[]{:S(2)}) collective-permute-start(f32[2,104,16,8]{1,3,2,0:T(8,128)} %copy.26), channel_id=1, source_target_pairs={{0,1},{1,2},{2,3},{3,4},{4,5},{5,6},{6,7},{7,8},{8,9},{9,10},{10,1... | collective-permute-start | bytes 319496 | tf_op jit(solution)/shard_map/ppermute | solution.py:14
  244.7 2.8 copy-start.4
where the time goes:
time: 300 us
  waiting for transfers between devices  155 us (52%)
  blocking collectives  46.3 us (15%)
  starting transfers between devices  42.7 us (14%)
  local copies, waits for them, and re-layouts  31.4 us (10%)
  matrix products  21.7 us (7%)
    ppermute x4, waiting for transfers between devices, with_halo(): after = lax.ppermute(first, axis, down)  74.9 us
    ppermute x4, waiting for transfers between devices, with_halo(): before = lax.ppermute(last, axis, up)  59.8 us
    all_to_all x1, blocking collectives, sent_and_summed(): pieces = lax.all_to_all(split_up(shard, dim, size), axis, 0, 0, tiled=True)  46.3 us
    all_to_all x1, starting transfers between devices, local(): lax.all_to_all(grad_tokens.reshape(channels, blocks, piece), ('lat', 'lon...  22.2 us
    all_to_all x1, waiting for transfers between devices, local(): lax.all_to_all(grad_tokens.reshape(channels, blocks, piece), ('lat', 'lon...  20.5 us
    ppermute x4, starting transfers between devices, with_halo(): before = lax.ppermute(last, axis, up)  12.1 us
    slice x6, local copies, waits for them, and re-layouts, with_halo(): last = lax.slice_in_dim(shard, length - width, length, axis=dim)  10.4 us
    dot_general x2, matrix products, localize(): jnp.einsum('mciu,uj->mcij', widened, lon_matrix, precision=lax.Precision....  9.82 us
  transfers between devices with their start and end apart: 9, of which 6 were waited for; matrix products, arithmetic and copies ran while one was open for 4% of the time, Pallas kernels for 0%

commit v1 on v0

v1 whole, which is shorter than its diff:
```python
import functools

import jax
import jax.numpy as jnp
from jax import lax
from jax.experimental import pallas as pl
from jax.experimental.pallas import tpu as pltpu
from jax.sharding import PartitionSpec as P

MESH = pl.DeviceIdType.MESH
BF16, F32 = jnp.bfloat16, jnp.float32
FIRST = (0, 4, 7, 10)
COUNT = (4, 3, 3, 3)
GROUP = 13
SLOTS = 4
ENS, LAT, LON = 8, 4, 16
ROWS, COLS = 16, 128
TALL = LAT * ROWS
HALO = 8
REACH = 2 * HALO
PIECE = 32
VMEM = pl.BlockSpec(memory_space=pltpu.VMEM)
ANY = pl.BlockSpec(memory_space=pl.ANY)
SMEM = pl.BlockSpec(memory_space=pltpu.SMEM)


def position():
    return lax.axis_index("ens"), lax.axis_index("lat"), lax.axis_index("lon")


def remote(src, dst, send, recv, device):
    return pltpu.make_async_remote_copy(
        src_ref=src, dst_ref=dst, send_sem=send, recv_sem=recv, device_id=device, device_id_type=MESH
    )


def first_of(lat):
    return jnp.where(lat == 0, 0, 3 * lat + 1)


def scatter_kernel(
    members, tok, index, order, moved_m, moved_t, moved_i,
    tile, sorted_t, m_send, m_recv, t_send, t_recv, u_send, u_recv, i_send, i_recv, own_sem,
):
    e, l, n = position()
    barrier = pltpu.get_barrier_semaphore()
    for de in range(ENS):
        for q in range(LAT):
            who = (lax.rem(e + de, ENS), q, n)
            if de == 0:

                @pl.when(l != q)
                def _():
                    pl.semaphore_signal(barrier, inc=1, device_id=who, device_id_type=MESH)
            else:
                pl.semaphore_signal(barrier, inc=1, device_id=who, device_id_type=MESH)
    for dn in range(1, LON):
        pl.semaphore_signal(barrier, inc=1, device_id=(e, l, lax.rem(n + dn, LON)), device_id_type=MESH)
    block = l * LON + n
    wanted = index[...]
    offset = (wanted >> 11) * PIECE + (wanted & 2047) - block * PIECE
    moved_i[l] = offset
    tile[n] = tok[n]

    @pl.when(l != 0)
    def _():
        moved_m[:, SLOTS - 1] = jnp.zeros((2 * ENS, LAT, ROWS, COLS), BF16)

    pl.semaphore_wait(barrier, ENS * LAT - 1 + LON - 1)

    def token_copy(dn):
        to = lax.rem(n + dn, LON)
        return remote(tok.at[to], tile.at[n], t_send.at[dn], t_recv.at[n], (e, l, to))

    for dn in range(1, LON):
        token_copy(dn).start()

    def index_copy(q):
        return remote(moved_i.at[l], moved_i.at[l], i_send.at[q], i_recv.at[l], (e, q, n))

    for q in range(LAT):

        @pl.when(l != q)
        def _():
            index_copy(q).start()

    def member_copy(de, q):
        to = lax.rem(e + de, ENS)
        return remote(
            members.at[:, pl.ds(GROUP * to + FIRST[q], COUNT[q])],
            moved_m.at[pl.ds(2 * e, 2), pl.ds(0, COUNT[q]), l],
            m_send.at[LAT * de + q],
            m_recv.at[LAT * e + l],
            (to, q, n),
        )

    def own_copy(q):
        return pltpu.make_async_copy(
            members.at[:, pl.ds(GROUP * e + FIRST[q], COUNT[q])],
            moved_m.at[pl.ds(2 * e, 2), pl.ds(0, COUNT[q]), l],
            own_sem.at[0],
        )

    for de in (4, 3, 5, 2, 6, 1, 7, 0):
        for q in range(LAT):
            if de == 0:

                @pl.when(l != q)
                def _():
                    member_copy(de, q).start()

                @pl.when(l == q)
                def _():
                    own_copy(q).start()
            else:
                member_copy(de, q).start()

    for dn in range(1, LON):
        frm = lax.rem(n + dn, LON)
        remote(tok.at[frm], tile.at[frm], t_send.at[dn], t_recv.at[frm], (e, l, frm)).wait_recv()
    flat = tile[...].reshape(LON * 16, COLS)
    sorted_t[...] = (
        jnp.dot(order[...], flat, preferred_element_type=F32).astype(BF16).reshape(LAT, 64, COLS)
    )
    moved_t[l] = sorted_t[l]

    def sorted_copy(q):
        return remote(sorted_t.at[q], moved_t.at[l], u_send.at[q], u_recv.at[l], (e, q, n))

    for q in range(LAT):

        @pl.when(l != q)
        def _():
            sorted_copy(q).start()

    for q in range(LAT):

        @pl.when(l != q)
        def _():
            remote(sorted_t.at[q], moved_t.at[q], u_send.at[q], u_recv.at[q], (e, q, n)).wait_recv()
            remote(moved_i.at[q], moved_i.at[q], i_send.at[q], i_recv.at[q], (e, q, n)).wait_recv()
            sorted_copy(q).wait_send()
            index_copy(q).wait_send()
    for dn in range(1, LON):
        token_copy(dn).wait_send()

    def arrival(frm, q, count):
        ref = moved_m.at[pl.ds(2 * frm, 2), pl.ds(0, count), q]
        return remote(ref, ref, m_send.at[0], m_recv.at[LAT * frm + q], (frm, q, n))

    for de in range(ENS):
        frm = lax.rem(e + de, ENS)
        for q in range(LAT):
            away = (l != q) if de == 0 else True

            @pl.when(jnp.logical_and(away, l == 0))
            def _():
                arrival(frm, q, COUNT[0]).wait_recv()

            @pl.when(jnp.logical_and(away, l != 0))
            def _():
                arrival(frm, q, COUNT[1]).wait_recv()

            if de == 0:

                @pl.when(l != q)
                def _():
                    member_copy(de, q).wait_send()

                @pl.when(l == q)
                def _():
                    own_copy(q).wait()
            else:
                member_copy(de, q).wait_send()


def scatter(members, tok, index, order):
    dma = pltpu.SemaphoreType.DMA
    return pl.pallas_call(
        scatter_kernel,
        out_shape=(
            jax.ShapeDtypeStruct((2 * ENS, SLOTS, LAT, ROWS, COLS), BF16),
            jax.ShapeDtypeStruct((LAT, 64, COLS), BF16),
            jax.ShapeDtypeStruct((LAT, ROWS, COLS), jnp.int32),
        ),
        in_specs=[ANY, VMEM, VMEM, VMEM],
        out_specs=(VMEM, VMEM, VMEM),
        scratch_shapes=[
            pltpu.VMEM((LON, 16, COLS), BF16),
            pltpu.VMEM((LAT, 64, COLS), BF16),
            dma((ENS * LAT,)), dma((ENS * LAT,)),
            dma((LON,)), dma((LON,)),
            dma((LAT,)), dma((LAT,)),
            dma((LAT,)), dma((LAT,)),
            dma((1,)),
        ],
        compiler_params=pltpu.CompilerParams(
            collective_id=0, has_side_effects=True, vmem_limit_bytes=40 * 2**20
        ),
    )(members, tok, index, order)


def iota(shape, dim):
    return lax.broadcasted_iota(jnp.int32, shape, dim)


def split(x):
    hi = x.astype(BF16)
    return hi, (x - hi.astype(F32)).astype(BF16)


def matrices(lat_taps, lon_taps, lat_hi, lat_lo, own_w, edge_hi, edge_lo):
    taps = [lat_taps[p] for p in range(2 * HALO + 1)]
    shift = iota((TALL, TALL), 1) - iota((TALL, TALL), 0) + HALO
    once = jnp.zeros((TALL, TALL), F32)
    for p, tap in enumerate(taps):
        once = jnp.where(shift == p, tap, once)
    both = lax.dot_general(
        once, once, (((1,), (1,)), ((), ())), precision=lax.Precision.HIGHEST, preferred_element_type=F32
    )
    hi, lo = split(both)
    lat_hi[...] = jnp.zeros_like(lat_hi)
    lat_lo[...] = jnp.zeros_like(lat_lo)
    for j in range(4):
        lat_hi[j * TALL : (j + 1) * TALL, j * TALL : (j + 1) * TALL] = hi
        lat_lo[j * TALL : (j + 1) * TALL, j * TALL : (j + 1) * TALL] = lo
    taps = [lon_taps[p] for p in range(2 * HALO + 1)]
    twice = []
    for d in range(REACH + 1):
        total = taps[d] * taps[0]
        for a in range(d + 1, REACH + 1):
            total = total + taps[a] * taps[a - d]
        twice.append(total)

    def band(distance):
        out = jnp.zeros(distance.shape, F32)
        for d in range(REACH + 1):
            out = jnp.where(distance == d, twice[d], out)
        return split(out)

    hi, lo = band(jnp.abs(iota((COLS, COLS), 0) - iota((COLS, COLS), 1)))
    own_w[0:COLS, 0:COLS] = hi
    own_w[COLS:, 0:COLS] = hi
    own_w[0:COLS, COLS:] = lo
    own_w[COLS:, COLS:] = jnp.zeros_like(lo)
    edge_hi[...] = jnp.zeros_like(edge_hi)
    edge_lo[...] = jnp.zeros_like(edge_lo)
    for side in range(2):
        start = -REACH if side == 0 else COLS
        hi, lo = band(jnp.abs(iota((REACH, COLS), 0) + start - iota((REACH, COLS), 1)))
        for j in range(8):
            rows = slice(side * COLS + j * REACH, side * COLS + (j + 1) * REACH)
            edge_hi[rows, j * COLS : (j + 1) * COLS] = hi
            edge_lo[rows, j * COLS : (j + 1) * COLS] = lo


def gather_kernel(
    moved_m, moved_t, moved_i, pack, spread, lat_taps, lon_taps,
    grid, edge_m, edge_g, lat_hi, lat_lo, own_w, edge_hi, edge_lo, lanes,
):
    matrices(lat_taps, lon_taps, lat_hi, lat_lo, own_w, edge_hi, edge_lo)
    parts = [moved_t[:, 16 * j : 16 * j + 16, :].astype(F32).reshape(64, COLS) for j in range(4)]
    lane = iota((64, COLS), 1) // PIECE
    for l in range(LAT):
        total = jnp.zeros((64, COLS), F32)
        for j in range(4):
            turned = parts[j] if j == l else pltpu.roll(parts[j], (j - l) * PIECE % COLS, 1)
            total = jnp.where(lane == j, turned, total)
        lanes[l] = total
    high = iota((8, COLS), 0) // 4
    for l in range(LAT):

        @pl.loop(0, ROWS)
        def _(i):
            offset = jnp.broadcast_to(moved_i[l, pl.ds(i, 1), :], (8, COLS))
            which = (offset >> 7) - high
            at = offset & 127
            total = jnp.zeros((8, COLS), F32)
            for v in range(8):
                found = jnp.take_along_axis(lanes[l, 8 * v : 8 * v + 8, :], at, axis=1)
                total = jnp.where(which == 2 * v, found, total)
            total = total[0:4] + total[4:8]
            for c in range(SLOTS):
                grid[c, pl.ds(l * ROWS + i, 1), :] = total[c : c + 1]

    for c in range(SLOTS):
        out = jnp.dot(grid[c].astype(BF16), spread[...], preferred_element_type=F32).astype(BF16)
        edge_g[0, c] = out[:, :COLS]
        edge_g[1, c] = out[:, COLS:]
        for half in range(2):
            row = jnp.concatenate(
                [moved_m[8 * half + j, c].reshape(TALL, COLS) for j in range(8)], axis=1
            )
            out = jnp.dot(row, pack[...], preferred_element_type=F32).astype(BF16)
            edge_m[0, 2 * c + half] = out[:, :COLS]
            edge_m[1, 2 * c + half] = out[:, COLS:]


def gathered(moved_m, moved_t, moved_i, pack, spread, lat_taps, lon_taps):
    s = jax.ShapeDtypeStruct
    return pl.pallas_call(
        gather_kernel,
        out_shape=(
            s((SLOTS, TALL, COLS), F32),
            s((2, 2 * SLOTS, TALL, COLS), BF16),
            s((2, SLOTS, TALL, COLS), BF16),
            s((256, 256), BF16), s((256, 256), BF16), s((256, 256), BF16),
            s((256, 1024), BF16), s((256, 1024), BF16),
        ),
        in_specs=[VMEM] * 5 + [SMEM] * 2,
        out_specs=(VMEM,) * 8,
        scratch_shapes=[pltpu.VMEM((LAT, 64, COLS), F32)],
        compiler_params=pltpu.CompilerParams(vmem_limit_bytes=40 * 2**20),
    )(moved_m, moved_t, moved_i, pack, spread, lat_taps, lon_taps)


def edge_kernel(edge_m, edge_g, near_m, near_g, send, recv):
    e, l, n = position()
    barrier = pltpu.get_barrier_semaphore()
    whom = [lax.rem(n + LON - 1, LON), lax.rem(n + 1, LON)]
    for to in whom:
        pl.semaphore_signal(barrier, inc=1, device_id=(e, l, to), device_id_type=MESH)
    pl.semaphore_wait(barrier, 2)
    copies = []
    for side in range(2):
        dev = (e, l, whom[side])
        copies.append(remote(edge_g.at[side], near_g.at[1 - side], send.at[side], recv.at[side], dev))
        copies.append(remote(edge_m.at[side], near_m.at[1 - side], send.at[2 + side], recv.at[2 + side], dev))
    for c in copies:
        c.start()
    for c in copies:
        c.wait()


def exchanged(edge_m, edge_g):
    s = jax.ShapeDtypeStruct
    return pl.pallas_call(
        edge_kernel,
        out_shape=(s(edge_m.shape, BF16), s(edge_g.shape, BF16)),
        in_specs=[VMEM] * 2,
        out_specs=(VMEM, VMEM),
        scratch_shapes=[pltpu.SemaphoreType.DMA((4,)), pltpu.SemaphoreType.DMA((4,))],
        compiler_params=pltpu.CompilerParams(
            collective_id=1, has_side_effects=True, vmem_limit_bytes=40 * 2**20
        ),
    )(edge_m, edge_g)


def local_kernel(moved_m, grid, near_m, near_g, lat_hi, lat_lo, own_w, edge_hi, edge_lo, out):
    def dot(a, b):
        return jnp.dot(a, b, preferred_element_type=F32)

    for c in range(SLOTS):
        g = grid[c]
        sides = [near_g[side, c].astype(F32) for side in range(2)]
        total = jnp.zeros((TALL, COLS), F32)
        for half in range(2):
            his, los = [], []
            for side in range(2):
                hi, lo = split(near_m[side, 2 * c + half].astype(F32) * sides[side])
                his.append(hi)
                los.append(lo)
            hi, lo = jnp.concatenate(his, axis=1), jnp.concatenate(los, axis=1)
            outer = dot(hi, edge_hi[...]) + dot(lo, edge_hi[...]) + dot(hi, edge_lo[...])
            z_hi, z_lo = [], []
            for j in range(8):
                m = moved_m[8 * half + j, c].reshape(TALL, COLS).astype(F32)
                hi, lo = split(m * g)
                both = dot(jnp.concatenate([hi, lo], axis=1), own_w[...])
                z = both[:, :COLS] + both[:, COLS:] + outer[:, j * COLS : (j + 1) * COLS]
                hi, lo = split(z)
                z_hi.append(hi)
                z_lo.append(lo)

            def field_pairs(parts):
                return jnp.concatenate(
                    [jnp.concatenate(parts[0:4], axis=0), jnp.concatenate(parts[4:8], axis=0)], axis=1
                )

            z_hi, z_lo = field_pairs(z_hi), field_pairs(z_lo)
            v = dot(lat_hi[...], z_hi) + dot(lat_lo[...], z_hi) + dot(lat_hi[...], z_lo)
            for j in range(8):
                m = moved_m[8 * half + j, c].reshape(TALL, COLS).astype(F32)
                k = j % 4
                total = total + m * v[k * TALL : (k + 1) * TALL, (j // 4) * COLS : (j // 4 + 1) * COLS]
        total = total / (2 * ENS - 1)
        for l in range(LAT):
            out[l, c] = total[l * ROWS : (l + 1) * ROWS]


def localized(*args):
    return pl.pallas_call(
        local_kernel,
        out_shape=jax.ShapeDtypeStruct((LAT, SLOTS, ROWS, COLS), F32),
        in_specs=[VMEM] * 9,
        out_specs=VMEM,
        compiler_params=pltpu.CompilerParams(vmem_limit_bytes=40 * 2**20),
    )(*args)


def return_kernel(part, out, send, recv):
    e, l, n = position()
    barrier = pltpu.get_barrier_semaphore()
    for q in range(LAT):

        @pl.when(l != q)
        def _():
            pl.semaphore_signal(barrier, inc=1, device_id=(e, q, n), device_id_type=MESH)

    pl.semaphore_wait(barrier, LAT - 1)

    def copy(src, q, count):
        return remote(
            part.at[q, pl.ds(0, count)], out.at[pl.ds(first_of(l), count)], send.at[q], recv.at[l], (e, q, n)
        )

    for q in range(LAT):
        for src in range(2):

            @pl.when(jnp.logical_and(l != q, (l != 0) if src else (l == 0)))
            def _():
                copy(src, q, COUNT[src]).start()

    for src in range(2):

        @pl.when((l != 0) if src else (l == 0))
        def _():
            out[pl.ds(first_of(l), COUNT[src])] = part[l, 0 : COUNT[src]]

    for q in range(LAT):

        @pl.when(l != q)
        def _():
            ref = out.at[pl.ds(FIRST[q], COUNT[q])]
            remote(ref, ref, send.at[q], recv.at[q], (e, q, n)).wait_recv()

        for src in range(2):

            @pl.when(jnp.logical_and(l != q, (l != 0) if src else (l == 0)))
            def _():
                copy(src, q, COUNT[src]).wait_send()


def returned(part):
    return pl.pallas_call(
        return_kernel,
        out_shape=jax.ShapeDtypeStruct((GROUP, ROWS, COLS), F32),
        in_specs=[VMEM],
        out_specs=VMEM,
        scratch_shapes=[pltpu.SemaphoreType.DMA((LAT,)), pltpu.SemaphoreType.DMA((LAT,))],
        compiler_params=pltpu.CompilerParams(collective_id=2, has_side_effects=True),
    )(part)


def selections():
    to, frm = jnp.arange(256)[:, None], jnp.arange(256)[None, :]
    q, j, g, ch = to // 64, to // 16 % 4, to // 4 % 4, to % 4
    order = (frm == (4 * g + j) * 16 + 4 * q + ch).astype(BF16)
    row, col = jnp.arange(1024)[:, None], jnp.arange(256)[None, :]
    side, j, cc = col // COLS, col % COLS // REACH, col % REACH
    edge = jnp.where(side == 0, cc, COLS - REACH + cc)
    pack = (row == j * COLS + edge).astype(BF16)
    spread = (jnp.arange(COLS)[:, None] == edge).astype(BF16)
    return order, pack, spread


def local(grad_tokens, token_index, members, lat_taps, lon_taps):
    e = lax.axis_index("ens")
    mine = lax.dynamic_slice_in_dim(grad_tokens, GROUP * e, GROUP, axis=0)
    rows = [FIRST[q] + min(c, COUNT[q] - 1) for q in range(LAT) for c in range(SLOTS)]
    mine = jnp.concatenate([mine[r : r + 1] for r in rows], axis=0)
    tok = mine.reshape(16, LAT, LON, PIECE).transpose(2, 0, 1, 3).reshape(LON, 16, COLS)
    order, pack, spread = selections()
    moved_m, moved_t, moved_i = scatter(members, tok, token_index, order)
    grid, edge_m, edge_g, *mats = gathered(moved_m, moved_t, moved_i, pack, spread, lat_taps, lon_taps)
    near_m, near_g = exchanged(edge_m, edge_g)
    part = localized(moved_m, grid, near_m, near_g, *mats)
    return returned(part)


def solution(mesh):
    in_specs = (P(None, ("lat", "lon")), P("lat", "lon"), P("ens", None, "lat", "lon"), P(), P())
    out_specs = P("ens", "lat", "lon")
    return jax.shard_map(local, mesh=mesh, in_specs=in_specs, out_specs=out_specs, check_vma=False)
```

time: 300 us -> 110 us (0.37)
  the two profiles are of different devices: /device:TPU:1 before, /device:TPU:33 now
where the time goes in v1:
time: 110 us; the launch traced here: 109 us
  Pallas kernels  102 us (93%)
  local copies, waits for them, and re-layouts  6.45 us (6%)
    pallas_call x1, Pallas kernels, scatter(): pl.pallas_call(scatter_kernel, out_shape=(jax.ShapeDtypeStruct((2 * ENS,...  63.6 us
    pallas_call x1, Pallas kernels, returned(): pl.pallas_call(return_kernel, out_shape=jax.ShapeDtypeStruct((GROUP, ROWS...  15.7 us
    pallas_call x1, Pallas kernels, exchanged(): pl.pallas_call(edge_kernel, out_shape=(s(edge_m.shape, BF16), s(edge_g.sh...  10.2 us
    pallas_call x1, Pallas kernels, gathered(): pl.pallas_call(gather_kernel, out_shape=(s((SLOTS, TALL, COLS), F32), s((...  7.35 us
    pallas_call x1, Pallas kernels, localized(): pl.pallas_call(local_kernel, out_shape=jax.ShapeDtypeStruct((LAT, SLOTS,...  5.28 us
    unnamed x11, local copies, waits for them, and re-layouts  3.39 us
    slice x3, local copies, waits for them, and re-layouts, local(): mine = jnp.concatenate([mine[r:r + 1] for r in rows], axis=0)  2.59 us

profile of v1, /device:TPU:33, one launch (start us, length us, event | category | flops | bytes accessed | tf_op | source)
XLA Modules:
  0.0 109.1 jit_solution(15268858745099241286)
XLA Ops:
  0.0 0.8 constant_dynamic-slice_fusion.3
  0.8 1.0 constant_dynamic-slice_fusion.1
  1.8 0.9 constant_dynamic-slice_fusion.2
  2.6 0.1 pad_maximum_fusion
  2.7 0.1 fusion.1.order
  2.8 0.0 copy-start
  2.8 0.2 reshape.274
  3.0 0.1 copy.8
  3.2 0.2 reshape.275.tok
  3.3 0.0 copy-start.2
  3.3 0.2 fusion.pack
  3.6 0.4 copy-done
  4.0 0.1 copy-done.2
  4.1 63.6 %shard_map.55 = (bf16[16,4,4,16,128]{4,3,2,1,0:T(8,128)(2,1)S(1)}, bf16[4,64,128]{2,1,0:T(8,128)(2,1)S(1)}, s32[4,16,128]{2,1,0:T(8,128)S(1)}) custom-call(bf16[2,104,16,128]{3,2,1,0:T(8,128)(2,1)S(1)} %copy-done, bf16[16,16,128]{2,1,0:T(8,128)(2,1)S(1)} %reshape.275.tok, s32[16,128]{1,0:T(8,128)S(1)} %copy-done.2, bf16[256,256]{1,0:T(8,128)(2,1)S(1)} %fusion.1.order), custom_call_target="tpu_custom_call" | custom-call | tf_op jit(solution)/shard_map/pallas_call | solution.py:179
  67.7 0.0 copy-start.3
  67.7 0.0 copy-start.4
  67.7 0.6 copy-done.3
  68.4 0.0 copy-done.4
  68.4 7.3 %shard_map.56 = (f32[4,64,128]{2,1,0:T(8,128)S(1)}, bf16[2,8,64,128]{3,2,1,0:T(8,128)(2,1)S(1)}, bf16[2,4,64,128]{3,2,1,0:T(8,128)(2,1)S(1)}, bf16[256,256]{1,0:...) custom-call(bf16[16,4,4,16,128]{4,3,2,1,0:T(8,128)(2,1)S(1)} %get-tu, ...), custom_call_target="tpu_custom_call" | custom-call | tf_op jit(solution)/shard_map/pallas_call | solution.py:301
  75.7 10.2 %shard_map.57 = (bf16[2,8,64,128]{3,2,1,0:T(8,128)(2,1)S(1)}, bf16[2,4,64,128]{3,2,1,0:T(8,128)(2,1)S(1)}) custom-call(bf16[2,8,64,128]{3,2,1,0:T(8,128)(2,1)S(1)} %get-tuple-element.22.edge_m, bf16[2,4,64,128]{3,2,1,0:T(8,128)(2,1)S(1)} %get-tuple-element.23.edge_g), custom_call_target="tpu_custom_call" | custom-call | tf_op jit(solution)/shard_map/pallas_call | solution.py:337
  85.9 5.3 %shard_map.58.part = f32[4,4,16,128]{3,2,1,0:T(8,128)S(1)} custom-call(bf16[16,4,4,16,128]{4,3,2,1,0:T(8,128)(2,1)S(1)} %get-tuple-element.18.moved_m, f32[4,64,128]{2,1,0:T(8,128)S(1)} %get-tuple-element.21.grid, bf16[2,8,64,128]{3,2,1,0:T(8,128)(2,1)S(1)} %get-tuple-element.24.near_m, bf16[2,4,64,128]{3,2,1,0:T(8,128)(2,1)S(1)} %get-tuple-element.25.near_g, ...), custom_call_target="tpu_custom_call" | custom-call | tf_op jit(solution)/shard_map/pallas_call | solution.py:392
  91.2 0.0 copy-start.1
  91.2 0.6 copy-done.1
  91.9 15.7 %shard_map.59 = f32[13,16,128]{2,1,0:T(8,128)} custom-call(f32[4,4,16,128]{3,2,1,0:T(8,128)} %copy-done.1), custom_call_target="tpu_custom_call" | custom-call | tf_op jit(solution)/shard_map/pallas_call | solution.py:445
  107.6 1.5 %copy.10 = f32[13,16,128]{2,1,0:T(8,128)} copy(f32[13,16,128]{2,1,0:T(8,128)} %shard_map.59) | data formatting | bytes 212992
  (3 shorter events, 0.0 us)
Async XLA Ops:
  2.8 1.2 %copy-start = (bf16[2,104,16,128]{3,2,1,0:T(8,128)(2,1)S(1)}, bf16[2,104,16,128]{3,2,1,0:T(8,128)(2,1)}, u32[]{:S(2)}) copy-start(bf16[2,104,16,128]{3,2,1,0:T(8,128)(2,1)} %members.1) | copy-start | bytes 2555908
  3.3 0.8 copy-start.2
  67.7 0.7 copy-start.3
  67.7 0.7 copy-start.4
  91.2 0.6 copy-start.1

commit v2 on v0

v2 whole, which is shorter than its diff:
```python
import functools

import jax
import jax.numpy as jnp
from jax import lax
from jax.experimental import pallas as pl
from jax.experimental.pallas import tpu as pltpu
from jax.sharding import PartitionSpec as P

MESH = pl.DeviceIdType.MESH
BF16, F32 = jnp.bfloat16, jnp.float32
FIRST = (0, 4, 7, 10)
COUNT = (4, 3, 3, 3)
CHANNELS = 104
GROUP = 13
SLOTS = 4
PART_FIRST = (0, 2)
PART_COUNT = ((2, 2, 2, 2), (2, 1, 1, 1))
ENS, LAT, LON = 8, 4, 16
ROWS, COLS = 16, 128
TALL = LAT * ROWS
HALO = 8
REACH = 2 * HALO
PIECE = 32
VMEM = pl.BlockSpec(memory_space=pltpu.VMEM)
ANY = pl.BlockSpec(memory_space=pl.ANY)
SMEM = pl.BlockSpec(memory_space=pltpu.SMEM)


def position():
    return lax.axis_index("ens"), lax.axis_index("lat"), lax.axis_index("lon")


def remote(src, dst, send, recv, device):
    return pltpu.make_async_remote_copy(
        src_ref=src, dst_ref=dst, send_sem=send, recv_sem=recv, device_id=device, device_id_type=MESH
    )


def first_of(lat):
    return jnp.where(lat == 0, 0, 3 * lat + 1)


def iota(shape, dim):
    return lax.broadcasted_iota(jnp.int32, shape, dim)


def split(x):
    hi = x.astype(BF16)
    return hi, (x - hi.astype(F32)).astype(BF16)


def matrices(lat_taps, lon_taps, lat_hi, lat_lo, own_w, edge_hi, edge_lo):
    taps = [lat_taps[p] for p in range(2 * HALO + 1)]
    shift = iota((TALL, TALL), 1) - iota((TALL, TALL), 0) + HALO
    once = jnp.zeros((TALL, TALL), F32)
    for p, tap in enumerate(taps):
        once = jnp.where(shift == p, tap, once)
    both = lax.dot_general(
        once, once, (((1,), (1,)), ((), ())), precision=lax.Precision.HIGHEST, preferred_element_type=F32
    )
    hi, lo = split(both)
    lat_hi[...] = jnp.zeros_like(lat_hi)
    lat_lo[...] = jnp.zeros_like(lat_lo)
    for j in range(4):
        lat_hi[j * TALL : (j + 1) * TALL, j * TALL : (j + 1) * TALL] = hi
        lat_lo[j * TALL : (j + 1) * TALL, j * TALL : (j + 1) * TALL] = lo
    taps = [lon_taps[p] for p in range(2 * HALO + 1)]
    twice = []
    for d in range(REACH + 1):
        total = taps[d] * taps[0]
        for a in range(d + 1, REACH + 1):
            total = total + taps[a] * taps[a - d]
        twice.append(total)

    def band(distance):
        out = jnp.zeros(distance.shape, F32)
        for d in range(REACH + 1):
            out = jnp.where(distance == d, twice[d], out)
        return split(out)

    hi, lo = band(jnp.abs(iota((COLS, COLS), 0) - iota((COLS, COLS), 1)))
    own_w[0:COLS, 0:COLS] = hi
    own_w[COLS:, 0:COLS] = hi
    own_w[0:COLS, COLS:] = lo
    own_w[COLS:, COLS:] = jnp.zeros_like(lo)
    edge_hi[...] = jnp.zeros_like(edge_hi)
    edge_lo[...] = jnp.zeros_like(edge_lo)
    for side in range(2):
        start = -REACH if side == 0 else COLS
        hi, lo = band(jnp.abs(iota((REACH, COLS), 0) + start - iota((REACH, COLS), 1)))
        for j in range(8):
            rows = slice(side * COLS + j * REACH, side * COLS + (j + 1) * REACH)
            edge_hi[rows, j * COLS : (j + 1) * COLS] = hi
            edge_lo[rows, j * COLS : (j + 1) * COLS] = lo


def kernel(
    members, grad, index, lat_taps, lon_taps, order, pack, spread, out,
    moved_m, tok, tile, sorted_t, moved_t, moved_i, lanes, grid, edge_m, edge_g, near_m, near_g,
    lat_hi, lat_lo, own_w, edge_hi, edge_lo, own_z, part,
    m_send, m_recv, t_send, t_recv, u_send, u_recv, i_send, i_recv, own_sem,
    g_send, g_recv, n_send, n_recv, r_send, r_recv,
):
    e, l, n = position()
    barrier = pltpu.get_barrier_semaphore()

    def greet(who):
        pl.semaphore_signal(barrier, inc=1, device_id=who, device_id_type=MESH)

    for de in (4, 3, 5, 2, 6, 1, 7, 0):
        for q in range(LAT):
            if de == 0:
                pl.when(l != q)(functools.partial(greet, (e, q, n)))
            else:
                greet((lax.rem(e + de, ENS), q, n))
    for dn in range(1, LON):
        greet((e, l, lax.rem(n + dn, LON)))

    lane = iota((16, COLS), 1) // PIECE
    row = iota((16, CHANNELS), 0)
    q, ch = row // 4, row % 4
    first = jnp.where(q == 0, 0, 3 * q + 1)
    ch = jnp.where(jnp.logical_and(q != 0, ch == 3), 2, ch)
    picks = (iota((16, CHANNELS), 1) == GROUP * e + first + ch).astype(F32).astype(BF16)
    mine = jnp.dot(picks, grad[...], preferred_element_type=F32)
    for g in range(4):
        tiles = [mine[:, (4 * q + g) * COLS : (4 * q + g + 1) * COLS] for q in range(LAT)]
        for j in range(4):
            total = jnp.zeros((16, COLS), F32)
            for q in range(LAT):
                turned = tiles[q] if q == j else pltpu.roll(tiles[q], (q - j) * PIECE % COLS, 1)
                total = jnp.where(lane == q, turned, total)
            tok[4 * g + j] = total.astype(BF16)
    wanted = index[...]
    moved_i[l] = (wanted >> 11) * PIECE + (wanted & 2047) - (l * LON + n) * PIECE
    tile[n] = tok[n]

    pl.semaphore_wait(barrier, ENS * LAT - 1 + LON - 1)

    def token_copy(dn):
        to = lax.rem(n + dn, LON)
        return remote(tok.at[to], tile.at[n], t_send.at[dn], t_recv.at[n], (e, l, to))

    def index_copy(q):
        return remote(moved_i.at[l], moved_i.at[l], i_send.at[q], i_recv.at[l], (e, q, n))

    def sorted_copy(q):
        return remote(sorted_t.at[q], moved_t.at[l], u_send.at[q], u_recv.at[l], (e, q, n))

    def member_refs(p, to, q):
        count = PART_COUNT[p][q]
        return (
            members.at[:, pl.ds(GROUP * to + FIRST[q] + PART_FIRST[p], count)],
            moved_m.at[pl.ds(2 * e, 2), pl.ds(PART_FIRST[p], count), l],
        )

    def member_copy(p, de, q):
        to = lax.rem(e + de, ENS)
        return remote(
            *member_refs(p, to, q), m_send.at[p, LAT * de + q], m_recv.at[p, LAT * e + l], (to, q, n)
        )

    def own_copy(p, q):
        return pltpu.make_async_copy(*member_refs(p, e, q), own_sem.at[p])

    def for_each(do, own=None):
        for de in (4, 3, 5, 2, 6, 1, 7, 0):
            for q in range(LAT):
                if de == 0:
                    pl.when(l != q)(functools.partial(do, de, q))
                    if own is not None:
                        pl.when(l == q)(functools.partial(own, q))
                else:
                    do(de, q)

    def others(do):
        for q in range(LAT):
            pl.when(l != q)(functools.partial(do, q))

    for dn in range(1, LON):
        token_copy(dn).start()
    others(lambda q: index_copy(q).start())
    for_each(lambda de, q: member_copy(0, de, q).start(), lambda q: own_copy(0, q).start())

    for dn in range(1, LON):
        frm = lax.rem(n + dn, LON)
        remote(tok.at[frm], tile.at[frm], t_send.at[dn], t_recv.at[frm], (e, l, frm)).wait_recv()
    flat = tile[...].reshape(LON * 16, COLS)
    sorted_t[...] = (
        jnp.dot(order[...], flat, preferred_element_type=F32).astype(BF16).reshape(LAT, 64, COLS)
    )
    moved_t[l] = sorted_t[l]
    others(lambda q: sorted_copy(q).start())

    matrices(lat_taps, lon_taps, lat_hi, lat_lo, own_w, edge_hi, edge_lo)

    def tokens_here(q):
        remote(sorted_t.at[q], moved_t.at[q], u_send.at[q], u_recv.at[q], (e, q, n)).wait_recv()
        remote(moved_i.at[q], moved_i.at[q], i_send.at[q], i_recv.at[q], (e, q, n)).wait_recv()
        sorted_copy(q).wait_send()
        index_copy(q).wait_send()

    others(tokens_here)
    for dn in range(1, LON):
        token_copy(dn).wait_send()

    parts = [moved_t[:, 16 * j : 16 * j + 16, :].astype(F32).reshape(64, COLS) for j in range(4)]
    lane = iota((64, COLS), 1) // PIECE
    for q in range(LAT):
        total = jnp.zeros((64, COLS), F32)
        for j in range(4):
            turned = parts[j] if j == q else pltpu.roll(parts[j], (j - q) * PIECE % COLS, 1)
            total = jnp.where(lane == j, turned, total)
        lanes[q] = total
    high = iota((8, COLS), 0) // 4

    @pl.loop(0, TALL)
    def _(i):
        q = i // ROWS
        offset = jnp.broadcast_to(moved_i[q, pl.ds(i % ROWS, 1), :], (8, COLS))
        which = (offset >> 7) - high
        at = offset & 127
        total = jnp.zeros((8, COLS), F32)
        for v in range(8):
            found = jnp.take_along_axis(lanes[q, 8 * v : 8 * v + 8, :], at, axis=1)
            total = jnp.where(which == 2 * v, found, total)
        total = total[0:4] + total[4:8]
        for c in range(SLOTS):
            grid[c, pl.ds(i, 1), :] = total[c : c + 1]

    for c in range(SLOTS):
        both = jnp.dot(grid[c].astype(BF16), spread[...], preferred_element_type=F32).astype(BF16)
        edge_g[0, c] = both[:, :COLS]
        edge_g[1, c] = both[:, COLS:]

    near = [(e, l, lax.rem(n + LON - 1, LON)), (e, l, lax.rem(n + 1, LON))]

    def grid_edge(side):
        return remote(edge_g.at[side], near_g.at[1 - side], g_send.at[side], g_recv.at[side], near[side])

    for side in range(2):
        grid_edge(side).start()

    def follow(de, q):
        member_copy(0, de, q).wait_send()
        member_copy(1, de, q).start()

    for_each(follow, lambda q: own_copy(1, q).start())

    def dot(a, b):
        return jnp.dot(a, b, preferred_element_type=F32)

    def member(c, m):
        return moved_m[m, c].reshape(TALL, COLS)

    def pack_edges(c, half):
        row = jnp.concatenate([member(c, 8 * half + j) for j in range(8)], axis=1)
        both = dot(row, pack[...]).astype(BF16)
        edge_m[0, 2 * c + half] = both[:, :COLS]
        edge_m[1, 2 * c + half] = both[:, COLS:]

    def own_columns(c, half):
        g = grid[c]
        his = []
        for j in range(8):
            hi, lo = split(member(c, 8 * half + j).astype(F32) * g)
            his.append(jnp.concatenate([hi, lo], axis=1))
        both = dot(jnp.concatenate(his, axis=0), own_w[...])
        own_z[c % 2, half] = both[:, :COLS] + both[:, COLS:]

    def finish(c, half):
        his, los = [], []
        for side in range(2):
            hi, lo = split(near_m[side, 2 * c + half].astype(F32) * near_g[side, c].astype(F32))
            his.append(hi)
            los.append(lo)
        hi, lo = jnp.concatenate(his, axis=1), jnp.concatenate(los, axis=1)
        outer = dot(hi, edge_hi[...]) + dot(lo, edge_hi[...]) + dot(hi, edge_lo[...])
        z_hi, z_lo = [], []
        for j in range(8):
            z = own_z[c % 2, half, j * TALL : (j + 1) * TALL] + outer[:, j * COLS : (j + 1) * COLS]
            hi, lo = split(z)
            z_hi.append(hi)
            z_lo.append(lo)

        def field_pairs(parts):
            return jnp.concatenate(
                [jnp.concatenate(parts[0:4], axis=0), jnp.concatenate(parts[4:8], axis=0)], axis=1
            )

        z_hi, z_lo = field_pairs(z_hi), field_pairs(z_lo)
        v = dot(lat_hi[...], z_hi) + dot(lat_lo[...], z_hi) + dot(lat_hi[...], z_lo)
        total = jnp.zeros((TALL, COLS), F32)
        for j in range(8):
            k = j % 4
            field = v[k * TALL : (k + 1) * TALL, (j // 4) * COLS : (j // 4 + 1) * COLS]
            total = total + member(c, 8 * half + j).astype(F32) * field
        return total

    def edge_copy(p, side, count):
        part_of = pl.ds(2 * PART_FIRST[p], 2 * count)
        return remote(
            edge_m.at[side, part_of], near_m.at[1 - side, part_of],
            n_send.at[p, side], n_recv.at[p, side], near[side],
        )

    def result_copy(p, q, count):
        return remote(
            part.at[q, pl.ds(PART_FIRST[p], count)],
            out.at[pl.ds(first_of(l) + PART_FIRST[p], count)],
            r_send.at[p, q], r_recv.at[p, l], (e, q, n),
        )

    def by_count(p, do):
        if PART_COUNT[p][0] == PART_COUNT[p][1]:
            do(PART_COUNT[p][0])
        else:
            pl.when(l == 0)(functools.partial(do, PART_COUNT[p][0]))
            pl.when(l != 0)(functools.partial(do, PART_COUNT[p][1]))

    def work(p, count):
        def arrived(de, q):
            frm = lax.rem(e + de, ENS)
            ref = moved_m.at[pl.ds(2 * frm, 2), pl.ds(PART_FIRST[p], count), q]
            remote(ref, ref, m_send.at[p, 0], m_recv.at[p, LAT * frm + q], (frm, q, n)).wait_recv()

        for_each(arrived, lambda q: own_copy(p, q).wait())
        slots = range(PART_FIRST[p], PART_FIRST[p] + count)
        for c in slots:
            for half in range(2):
                pack_edges(c, half)
        for side in range(2):
            edge_copy(p, side, count).start()
        for c in slots:
            for half in range(2):
                own_columns(c, half)
        for side in range(2):
            if p == 0:
                grid_edge(side).wait()
            edge_copy(p, side, count).wait()
        for c in slots:
            total = finish(c, 0) + finish(c, 1)
            for q in range(LAT):
                part[q, c] = total[q * ROWS : (q + 1) * ROWS]
        others(lambda q: result_copy(p, q, count).start())
        out[pl.ds(first_of(l) + PART_FIRST[p], count)] = part[l, pl.ds(PART_FIRST[p], count)]

    for p in range(2):
        by_count(p, functools.partial(work, p))

    for_each(lambda de, q: member_copy(1, de, q).wait_send())
    for p in range(2):

        def result_here(q, p=p):
            ref = out.at[pl.ds(FIRST[q] + PART_FIRST[p], PART_COUNT[p][q])]
            remote(ref, ref, r_send.at[p, q], r_recv.at[p, q], (e, q, n)).wait_recv()

        others(result_here)
        by_count(p, lambda count, p=p: others(lambda q: result_copy(p, q, count).wait_send()))


def increments(members, grad, index, lat_taps, lon_taps, order, pack, spread):
    dma = pltpu.SemaphoreType.DMA
    return pl.pallas_call(
        kernel,
        out_shape=jax.ShapeDtypeStruct((GROUP, ROWS, COLS), F32),
        in_specs=[ANY, VMEM, VMEM, SMEM, SMEM, VMEM, VMEM, VMEM],
        out_specs=VMEM,
        scratch_shapes=[
            pltpu.VMEM((2 * ENS, SLOTS, LAT, ROWS, COLS), BF16),
            pltpu.VMEM((LON, 16, COLS), BF16),
            pltpu.VMEM((LON, 16, COLS), BF16),
            pltpu.VMEM((LAT, 64, COLS), BF16),
            pltpu.VMEM((LAT, 64, COLS), BF16),
            pltpu.VMEM((LAT, ROWS, COLS), jnp.int32),
            pltpu.VMEM((LAT, 64, COLS), F32),
            pltpu.VMEM((SLOTS, TALL, COLS), F32),
            pltpu.VMEM((2, 2 * SLOTS, TALL, COLS), BF16),
            pltpu.VMEM((2, SLOTS, TALL, COLS), BF16),
            pltpu.VMEM((2, 2 * SLOTS, TALL, COLS), BF16),
            pltpu.VMEM((2, SLOTS, TALL, COLS), BF16),
            pltpu.VMEM((256, 256), BF16),
            pltpu.VMEM((256, 256), BF16),
            pltpu.VMEM((256, 256), BF16),
            pltpu.VMEM((256, 1024), BF16),
            pltpu.VMEM((256, 1024), BF16),
            pltpu.VMEM((2, 2, 8 * TALL, COLS), F32),
            pltpu.VMEM((LAT, SLOTS, ROWS, COLS), F32),
            dma((2, ENS * LAT)), dma((2, ENS * LAT)),
            dma((LON,)), dma((LON,)),
            dma((LAT,)), dma((LAT,)),
            dma((LAT,)), dma((LAT,)),
            dma((2,)),
            dma((2,)), dma((2,)),
            dma((2, 2)), dma((2, 2)),
            dma((2, LAT)), dma((2, LAT)),
        ],
        compiler_params=pltpu.CompilerParams(
            collective_id=0, has_side_effects=True, vmem_limit_bytes=48 * 2**20
        ),
    )(members, grad, index, lat_taps, lon_taps, order, pack, spread)


def selections():
    to, frm = jnp.arange(256)[:, None], jnp.arange(256)[None, :]
    q, j, g, ch = to // 64, to // 16 % 4, to // 4 % 4, to % 4
    order = (frm == (4 * g + j) * 16 + 4 * q + ch).astype(BF16)
    row, col = jnp.arange(1024)[:, None], jnp.arange(256)[None, :]
    side, j, cc = col // COLS, col % COLS // REACH, col % REACH
    edge = jnp.where(side == 0, cc, COLS - REACH + cc)
    pack = (row == j * COLS + edge).astype(BF16)
    spread = (jnp.arange(COLS)[:, None] == edge).astype(BF16)
    return order, pack, spread


def local(grad_tokens, token_index, members, lat_taps, lon_taps):
    order, pack, spread = selections()
    total = increments(members, grad_tokens, token_index, lat_taps, lon_taps, order, pack, spread)
    return total / (2 * ENS - 1)


def solution(mesh):
    in_specs = (P(None, ("lat", "lon")), P("lat", "lon"), P("ens", None, "lat", "lon"), P(), P())
    out_specs = P("ens", "lat", "lon")
    return jax.shard_map(local, mesh=mesh, in_specs=in_specs, out_specs=out_specs, check_vma=False)
```

time: 300 us -> 91.9 us (0.31)
  waiting for transfers between devices: 155 us -> 0 us
  Pallas kernels: 0 us -> 88.8 us
  blocking collectives: 46.3 us -> 0 us
  starting transfers between devices: 42.7 us -> 0 us
  local copies, waits for them, and re-layouts: 31.4 us -> 1.76 us
  matrix products: 21.7 us -> 0 us
    ppermute x8 -> x0, waiting for transfers between devices: 135 us -> none  [the longest x4 74.9 us: with_halo(): after = lax.ppermute(first, axis, down)]
    pallas_call x0 -> x1, Pallas kernels: none -> 88.8 us  [increments(): pl.pallas_call(kernel, out_shape=jax.ShapeDtypeStruct((GROUP, ROWS, COLS)...]
    all_to_all x1 -> x0, blocking collectives: 46.3 us -> none  [sent_and_summed(): pieces = lax.all_to_all(split_up(shard, dim, size), axis, 0, 0, tiled=True)]
    all_to_all x1 -> x0, starting transfers between devices: 22.2 us -> none  [local(): lax.all_to_all(grad_tokens.reshape(channels, blocks, piece), ('lat', 'lon...]
    dot_general x8 -> x0, matrix products: 21.7 us -> none  [the longest x2 9.82 us: localize(): jnp.einsum('mciu,uj->mcij', widened, lon_matrix, precision=lax.Precision....]
    all_to_all x1 -> x0, waiting for transfers between devices: 20.5 us -> none  [local(): lax.all_to_all(grad_tokens.reshape(channels, blocks, piece), ('lat', 'lon...]
    ppermute x8 -> x0, starting transfers between devices: 20.4 us -> none  [the longest x4 12.1 us: with_halo(): before = lax.ppermute(last, axis, up)]
    slice x8 -> x0, local copies, waits for them, and re-layouts: 11.7 us -> none  [the longest x6 10.4 us: with_halo(): last = lax.slice_in_dim(shard, length - width, length, axis=dim)]
  transfers between devices with their start and end apart: 9 -> 0, of which waited for: 6 -> 0; matrix products, arithmetic and copies ran while one was open for 4% -> 0% of each run, Pallas kernels for 0% -> 0%
where the time goes in v2:
time: 91.9 us; the launch traced here: 91.6 us
  Pallas kernels  88.8 us (97%)
  local copies, waits for them, and re-layouts  1.76 us (2%)
  other arithmetic  1.01 us (1%)
    pallas_call x1, Pallas kernels, increments(): pl.pallas_call(kernel, out_shape=jax.ShapeDtypeStruct((GROUP, ROWS, COLS)...  88.8 us

profile of v2, /device:TPU:1, one launch (start us, length us, event | category | flops | bytes accessed | tf_op | source)
XLA Modules:
  0.0 91.6 jit_solution(11249558872886786823)
XLA Ops:
  0.0 0.0 copy-start.1
  0.1 0.1 fusion.1.order
  0.2 0.0 copy-start.2
  0.2 0.0 copy-start.3
  0.2 0.0 copy-start.4
  0.2 0.2 fusion.pack
  0.4 0.6 copy-done.1
  1.0 0.0 copy-done.2
  1.0 0.0 copy-done.3
  1.0 0.0 copy-done.4
  1.0 0.0 copy-start
  1.0 1.1 %copy-done = bf16[2,104,16,128]{3,2,1,0:T(8,128)(2,1)S(1)} copy-done((bf16[2,104,16,128]{3,2,1,0:T(8,128)(2,1)S(1)}, bf16[2,104,16,128]{3,2,1,0:T(8,128)(2,1)}, u32[]{:S(2)}) %copy-start) | copy-done | bytes 851992
  2.2 88.8 %shard_map.55 = f32[13,16,128]{2,1,0:T(8,128)S(1)} custom-call(bf16[2,104,16,128]{3,2,1,0:T(8,128)(2,1)S(1)} %copy-done, bf16[104,2048]{1,0:T(8,128)(2,1)S(1)} %copy-done.1, s32[16,128]{1,0:T(8,128)S(1)} %copy-done.2, f32[17]{0:T(128)S(1)} %copy-done.3, f32[17]{0:T(128)S(1)} %copy-done.4, bf16[256,256]{1,0:T(8,128)(2,1)S(1)} %fusion.1.order, ...), custom_call_target="tpu_custom_call" | custom-call | tf_op jit(solution)/shard_map/pallas_call | solution.py:365
  90.9 0.7 broadcast_multiply_fusion
  (4 shorter events, 0.0 us)
Async XLA Ops:
  0.0 1.0 %copy-start.1 = (bf16[104,2048]{1,0:T(8,128)(2,1)S(1)}, bf16[104,2048]{1,0:T(8,128)(2,1)}, u32[]{:S(2)}) copy-start(bf16[104,2048]{1,0:T(8,128)(2,1)} %grad.1) | copy-start | bytes 1277956
  0.2 0.8 copy-start.2
  0.2 0.8 copy-start.3
  0.2 0.8 copy-start.4
  1.0 1.2 %copy-start = (bf16[2,104,16,128]{3,2,1,0:T(8,128)(2,1)S(1)}, bf16[2,104,16,128]{3,2,1,0:T(8,128)(2,1)}, u32[]{:S(2)}) copy-start(bf16[2,104,16,128]{3,2,1,0:T(8,128)(2,1)} %members.1) | copy-start | bytes 2555908

commit v3 on v2

--- a/solution.py
+++ b/solution.py
@@ -9,13 +9,12 @@
 
 MESH = pl.DeviceIdType.MESH
 BF16, F32 = jnp.bfloat16, jnp.float32
-FIRST = (0, 4, 7, 10)
-COUNT = (4, 3, 3, 3)
 CHANNELS = 104
 GROUP = 13
 SLOTS = 4
-PART_FIRST = (0, 2)
-PART_COUNT = ((2, 2, 2, 2), (2, 1, 1, 1))
+SPARE = 2
+DEPTH = 16
+OFFSETS = (8, 7, 9, 6, 10, 5, 11, 4, 12, 3, 13, 2, 14, 1, 15, 0)
 ENS, LAT, LON = 8, 4, 16
 ROWS, COLS = 16, 128
 TALL = LAT * ROWS
@@ -95,35 +94,120 @@
             edge_lo[rows, j * COLS : (j + 1) * COLS] = lo
 
 
+def token_order(order):
+    to, frm = iota((256, 256), 0), iota((256, 256), 1)
+    q, j, g, ch = to // 64, to // 16 % 4, to // 4 % 4, to % 4
+    order[...] = (frm == (4 * g + j) * 16 + 4 * q + ch).astype(F32).astype(BF16)
+
+
+def edge_selections(pack, spread):
+    col = iota((COLS, 256), 1)
+    side, j, cc = col // COLS, col % COLS // REACH, col % REACH
+    edge = jnp.where(side == 0, cc, COLS - REACH + cc)
+    hit = iota((COLS, 256), 0) == edge
+    spread[...] = hit.astype(F32).astype(BF16)
+    for k in range(8):
+        here = jnp.logical_and(hit, j == k)
+        pack[k * COLS : (k + 1) * COLS] = here.astype(F32).astype(BF16)
+
+
 def kernel(
-    members, grad, index, lat_taps, lon_taps, order, pack, spread, out,
-    moved_m, tok, tile, sorted_t, moved_t, moved_i, lanes, grid, edge_m, edge_g, near_m, near_g,
+    members, grad, index, lat_taps, lon_taps, out,
+    tokens_in, index_in, order, pack, spread, moved_m, tok, tile, sorted_t, moved_t, moved_i, lanes, grid, edge_m, edge_g, near_m, near_g,
     lat_hi, lat_lo, own_w, edge_hi, edge_lo, own_z, part,
-    m_send, m_recv, t_send, t_recv, u_send, u_recv, i_send, i_recv, own_sem,
+    m_send, m_recv, s_send, s_recv, t_send, t_recv, u_send, u_recv, i_send, i_recv, own_sem,
     g_send, g_recv, n_send, n_recv, r_send, r_recv,
 ):
     e, l, n = position()
+    core = lax.rem(l, 2)
+    z = (l // 2) * ENS + e
     barrier = pltpu.get_barrier_semaphore()
+
+    def along(d, kk):
+        there = lax.rem(z + d, DEPTH)
+        return lax.rem(there, ENS), 2 * (there // ENS) + lax.rem(core + kk, 2)
 
     def greet(who):
         pl.semaphore_signal(barrier, inc=1, device_id=who, device_id_type=MESH)
 
-    for de in (4, 3, 5, 2, 6, 1, 7, 0):
-        for q in range(LAT):
-            if de == 0:
-                pl.when(l != q)(functools.partial(greet, (e, q, n)))
-            else:
-                greet((lax.rem(e + de, ENS), q, n))
+    pairs = [(d, kk) for d in OFFSETS for kk in range(2) if (d, kk) != (0, 0)]
+    for d, kk in pairs:
+        greet((*along(d, kk), n))
     for dn in range(1, LON):
         greet((e, l, lax.rem(n + dn, LON)))
-
+    read_grad = pltpu.make_async_copy(grad, tokens_in, own_sem.at[3])
+    read_index = pltpu.make_async_copy(index, index_in, own_sem.at[4])
+    read_grad.start()
+    read_index.start()
+
+    pl.semaphore_wait(barrier, ENS * LAT - 1 + LON - 1)
+
+    def token_copy(dn):
+        to = lax.rem(n + dn, LON)
+        return remote(tok.at[to], tile.at[n], t_send.at[dn], t_recv.at[n], (e, l, to))
+
+    def index_copy(q):
+        return remote(moved_i.at[l], moved_i.at[l], i_send.at[q], i_recv.at[l], (e, q, n))
+
+    def sorted_copy(q):
+        return remote(sorted_t.at[q], moved_t.at[l], u_send.at[q], u_recv.at[l], (e, q, n))
+
+    def member_refs(p, to, q):
+        slot, channel, count = ((0, 0, 2), (3, jnp.where(q == 0, 3, 2), 1), (SPARE, SPARE, 1))[p]
+        return (
+            members.at[:, pl.ds(GROUP * to + first_of(q) + channel, count)],
+            moved_m.at[pl.ds(2 * e, 2), pl.ds(slot, count), l],
+        )
+
+    def member_copy(p, d, kk):
+        to, q = along(d, kk)
+        return remote(*member_refs(p, to, q), m_send.at[p, 2 * d + kk], m_recv.at[p, 2 * d + kk], (to, q, n))
+
+    def member_here(p, d, kk):
+        frm, q = along(DEPTH - d, kk)
+        slot, count = ((0, 2), (3, 1))[p]
+        ref = moved_m.at[pl.ds(2 * frm, 2), pl.ds(slot, count), q]
+        return remote(ref, ref, m_send.at[p, 2 * d + kk], m_recv.at[p, 2 * d + kk], (frm, q, n))
+
+    def own_copy(p):
+        return pltpu.make_async_copy(*member_refs(p, e, l), own_sem.at[p])
+
+    def send_part(p):
+        for d, kk in pairs:
+            member_copy(p, d, kk).start()
+        own_copy(p).start()
+
+    def spare_copy(de):
+        to = lax.rem(e + de, ENS)
+        return remote(*member_refs(2, to, 0), s_send.at[de], s_recv.at[de, l], (to, 0, n))
+
+    def spare_here(de, q):
+        frm = lax.rem(e + ENS - de, ENS)
+        ref = moved_m.at[pl.ds(2 * frm, 2), pl.ds(SPARE, 1), q]
+        return remote(ref, ref, s_send.at[de], s_recv.at[de, q], (frm, q, n))
+
+    def own_spare():
+        return pltpu.make_async_copy(*member_refs(2, e, 0), own_sem.at[2])
+
+    def for_spares(do):
+        for de in (4, 3, 5, 2, 6, 1, 7):
+            do(de)
+        pl.when(l != 0)(functools.partial(do, 0))
+
+    def others(do):
+        for q in range(LAT):
+            pl.when(l != q)(functools.partial(do, q))
+
+    send_part(0)
     lane = iota((16, COLS), 1) // PIECE
     row = iota((16, CHANNELS), 0)
     q, ch = row // 4, row % 4
     first = jnp.where(q == 0, 0, 3 * q + 1)
     ch = jnp.where(jnp.logical_and(q != 0, ch == 3), 2, ch)
     picks = (iota((16, CHANNELS), 1) == GROUP * e + first + ch).astype(F32).astype(BF16)
-    mine = jnp.dot(picks, grad[...], preferred_element_type=F32)
+    read_grad.wait()
+    read_index.wait()
+    mine = jnp.dot(picks, tokens_in[...], preferred_element_type=F32)
     for g in range(4):
         tiles = [mine[:, (4 * q + g) * COLS : (4 * q + g + 1) * COLS] for q in range(LAT)]
         for j in range(4):
@@ -132,57 +216,15 @@
                 turned = tiles[q] if q == j else pltpu.roll(tiles[q], (q - j) * PIECE % COLS, 1)
                 total = jnp.where(lane == q, turned, total)
             tok[4 * g + j] = total.astype(BF16)
-    wanted = index[...]
+    wanted = index_in[...]
     moved_i[l] = (wanted >> 11) * PIECE + (wanted & 2047) - (l * LON + n) * PIECE
     tile[n] = tok[n]
-
-    pl.semaphore_wait(barrier, ENS * LAT - 1 + LON - 1)
-
-    def token_copy(dn):
-        to = lax.rem(n + dn, LON)
-        return remote(tok.at[to], tile.at[n], t_send.at[dn], t_recv.at[n], (e, l, to))
-
-    def index_copy(q):
-        return remote(moved_i.at[l], moved_i.at[l], i_send.at[q], i_recv.at[l], (e, q, n))
-
-    def sorted_copy(q):
-        return remote(sorted_t.at[q], moved_t.at[l], u_send.at[q], u_recv.at[l], (e, q, n))
-
-    def member_refs(p, to, q):
-        count = PART_COUNT[p][q]
-        return (
-            members.at[:, pl.ds(GROUP * to + FIRST[q] + PART_FIRST[p], count)],
-            moved_m.at[pl.ds(2 * e, 2), pl.ds(PART_FIRST[p], count), l],
-        )
-
-    def member_copy(p, de, q):
-        to = lax.rem(e + de, ENS)
-        return remote(
-            *member_refs(p, to, q), m_send.at[p, LAT * de + q], m_recv.at[p, LAT * e + l], (to, q, n)
-        )
-
-    def own_copy(p, q):
-        return pltpu.make_async_copy(*member_refs(p, e, q), own_sem.at[p])
-
-    def for_each(do, own=None):
-        for de in (4, 3, 5, 2, 6, 1, 7, 0):
-            for q in range(LAT):
-                if de == 0:
-                    pl.when(l != q)(functools.partial(do, de, q))
-                    if own is not None:
-                        pl.when(l == q)(functools.partial(own, q))
-                else:
-                    do(de, q)
-
-    def others(do):
-        for q in range(LAT):
-            pl.when(l != q)(functools.partial(do, q))
 
     for dn in range(1, LON):
         token_copy(dn).start()
     others(lambda q: index_copy(q).start())
-    for_each(lambda de, q: member_copy(0, de, q).start(), lambda q: own_copy(0, q).start())
-
+
+    token_order(order)
     for dn in range(1, LON):
         frm = lax.rem(n + dn, LON)
         remote(tok.at[frm], tile.at[frm], t_send.at[dn], t_recv.at[frm], (e, l, frm)).wait_recv()
@@ -192,7 +234,11 @@
     )
     moved_t[l] = sorted_t[l]
     others(lambda q: sorted_copy(q).start())
-
+    for_spares(lambda de: spare_copy(de).start())
+    pl.when(l == 0)(lambda: own_spare().start())
+    send_part(1)
+
+    edge_selections(pack, spread)
     matrices(lat_taps, lon_taps, lat_hi, lat_lo, own_w, edge_hi, edge_lo)
 
     def tokens_here(q):
@@ -215,7 +261,7 @@
         lanes[q] = total
     high = iota((8, COLS), 0) // 4
 
-    @pl.loop(0, TALL)
+    @pl.loop(0, TALL, unroll=8)
     def _(i):
         q = i // ROWS
         offset = jnp.broadcast_to(moved_i[q, pl.ds(i % ROWS, 1), :], (8, COLS))
@@ -242,12 +288,6 @@
     for side in range(2):
         grid_edge(side).start()
 
-    def follow(de, q):
-        member_copy(0, de, q).wait_send()
-        member_copy(1, de, q).start()
-
-    for_each(follow, lambda q: own_copy(1, q).start())
-
     def dot(a, b):
         return jnp.dot(a, b, preferred_element_type=F32)
 
@@ -267,7 +307,7 @@
             hi, lo = split(member(c, 8 * half + j).astype(F32) * g)
             his.append(jnp.concatenate([hi, lo], axis=1))
         both = dot(jnp.concatenate(his, axis=0), own_w[...])
-        own_z[c % 2, half] = both[:, :COLS] + both[:, COLS:]
+        own_z[c, half] = both[:, :COLS] + both[:, COLS:]
 
     def finish(c, half):
         his, los = [], []
@@ -279,7 +319,7 @@
         outer = dot(hi, edge_hi[...]) + dot(lo, edge_hi[...]) + dot(hi, edge_lo[...])
         z_hi, z_lo = [], []
         for j in range(8):
-            z = own_z[c % 2, half, j * TALL : (j + 1) * TALL] + outer[:, j * COLS : (j + 1) * COLS]
+            z = own_z[c, half, j * TALL : (j + 1) * TALL] + outer[:, j * COLS : (j + 1) * COLS]
             hi, lo = split(z)
             z_hi.append(hi)
             z_lo.append(lo)
@@ -298,76 +338,104 @@
             total = total + member(c, 8 * half + j).astype(F32) * field
         return total
 
-    def edge_copy(p, side, count):
-        part_of = pl.ds(2 * PART_FIRST[p], 2 * count)
+    def edge_copy(p, side):
+        part_of = (pl.ds(0, 4), pl.ds(6, 2), pl.ds(4, 2))[p]
         return remote(
             edge_m.at[side, part_of], near_m.at[1 - side, part_of],
             n_send.at[p, side], n_recv.at[p, side], near[side],
         )
 
-    def result_copy(p, q, count):
-        return remote(
-            part.at[q, pl.ds(PART_FIRST[p], count)],
-            out.at[pl.ds(first_of(l) + PART_FIRST[p], count)],
-            r_send.at[p, q], r_recv.at[p, l], (e, q, n),
-        )
-
-    def by_count(p, do):
-        if PART_COUNT[p][0] == PART_COUNT[p][1]:
-            do(PART_COUNT[p][0])
-        else:
-            pl.when(l == 0)(functools.partial(do, PART_COUNT[p][0]))
-            pl.when(l != 0)(functools.partial(do, PART_COUNT[p][1]))
-
-    def work(p, count):
-        def arrived(de, q):
-            frm = lax.rem(e + de, ENS)
-            ref = moved_m.at[pl.ds(2 * frm, 2), pl.ds(PART_FIRST[p], count), q]
-            remote(ref, ref, m_send.at[p, 0], m_recv.at[p, LAT * frm + q], (frm, q, n)).wait_recv()
-
-        for_each(arrived, lambda q: own_copy(p, q).wait())
-        slots = range(PART_FIRST[p], PART_FIRST[p] + count)
+    def result_refs(p, frm, to):
+        slot, channel, count = ((0, 0, 2), (3, jnp.where(frm == 0, 3, 2), 1), (SPARE, SPARE, 1))[p]
+        return part.at[to, pl.ds(slot, count)], out.at[pl.ds(first_of(frm) + channel, count)]
+
+    def result_copy(p, q):
+        return remote(*result_refs(p, l, q), r_send.at[p, q], r_recv.at[p, l], (e, q, n))
+
+    def result_here(p, q):
+        ref = result_refs(p, jnp.int32(q), l)[1]
+        return remote(ref, ref, r_send.at[p, q], r_recv.at[p, q], (e, q, n))
+
+    def begin(p, slots):
         for c in slots:
             for half in range(2):
                 pack_edges(c, half)
         for side in range(2):
-            edge_copy(p, side, count).start()
+            edge_copy(p, side).start()
+
+    def middle(slots):
         for c in slots:
             for half in range(2):
                 own_columns(c, half)
+
+    def complete(p, slots):
         for side in range(2):
-            if p == 0:
-                grid_edge(side).wait()
-            edge_copy(p, side, count).wait()
+            edge_copy(p, side).wait()
         for c in slots:
             total = finish(c, 0) + finish(c, 1)
             for q in range(LAT):
                 part[q, c] = total[q * ROWS : (q + 1) * ROWS]
-        others(lambda q: result_copy(p, q, count).start())
-        out[pl.ds(first_of(l) + PART_FIRST[p], count)] = part[l, pl.ds(PART_FIRST[p], count)]
-
+        others(lambda q: result_copy(p, q).start())
+        to = result_refs(p, l, l)[1]
+        to[...] = part[l, slots[0] : slots[-1] + 1]
+
+    for d, kk in pairs:
+        member_here(0, d, kk).wait_recv()
+    own_copy(0).wait()
+    begin(0, (0, 1))
+
+    @pl.when(l == 0)
+    def _():
+        for de in range(ENS):
+            for q in range(LAT):
+                if (de, q) != (0, 0):
+                    spare_here(de, q).wait_recv()
+        own_spare().wait()
+        begin(2, (SPARE,))
+
+    middle((0, 1))
+    for side in range(2):
+        grid_edge(side).wait()
+    for d, kk in pairs:
+        member_here(1, d, kk).wait_recv()
+    own_copy(1).wait()
+    begin(1, (3,))
+    complete(0, (0, 1))
+
+    @pl.when(l == 0)
+    def _():
+        middle((SPARE,))
+        complete(2, (SPARE,))
+
+    middle((3,))
     for p in range(2):
-        by_count(p, functools.partial(work, p))
-
-    for_each(lambda de, q: member_copy(1, de, q).wait_send())
+        for d, kk in pairs:
+            member_copy(p, d, kk).wait_send()
+    for_spares(lambda de: spare_copy(de).wait_send())
+    complete(1, (3,))
     for p in range(2):
-
-        def result_here(q, p=p):
-            ref = out.at[pl.ds(FIRST[q] + PART_FIRST[p], PART_COUNT[p][q])]
-            remote(ref, ref, r_send.at[p, q], r_recv.at[p, q], (e, q, n)).wait_recv()
-
-        others(result_here)
-        by_count(p, lambda count, p=p: others(lambda q: result_copy(p, q, count).wait_send()))
-
-
-def increments(members, grad, index, lat_taps, lon_taps, order, pack, spread):
+        others(lambda q, p=p: result_here(p, q).wait_recv())
+        others(lambda q, p=p: result_copy(p, q).wait_send())
+    pl.when(l != 0)(lambda: result_here(2, 0).wait_recv())
+
+    @pl.when(l == 0)
+    def _():
+        others(lambda q: result_copy(2, q).wait_send())
+
+
+def increments(members, grad, index, lat_taps, lon_taps):
     dma = pltpu.SemaphoreType.DMA
     return pl.pallas_call(
         kernel,
         out_shape=jax.ShapeDtypeStruct((GROUP, ROWS, COLS), F32),
-        in_specs=[ANY, VMEM, VMEM, SMEM, SMEM, VMEM, VMEM, VMEM],
+        in_specs=[ANY, ANY, ANY, SMEM, SMEM],
         out_specs=VMEM,
         scratch_shapes=[
+            pltpu.VMEM((CHANNELS, ROWS * COLS), BF16),
+            pltpu.VMEM((ROWS, COLS), jnp.int32),
+            pltpu.VMEM((256, 256), BF16),
+            pltpu.VMEM((1024, 256), BF16),
+            pltpu.VMEM((COLS, 256), BF16),
             pltpu.VMEM((2 * ENS, SLOTS, LAT, ROWS, COLS), BF16),
             pltpu.VMEM((LON, 16, COLS), BF16),
             pltpu.VMEM((LON, 16, COLS), BF16),
@@ -385,38 +453,26 @@
             pltpu.VMEM((256, 256), BF16),
             pltpu.VMEM((256, 1024), BF16),
             pltpu.VMEM((256, 1024), BF16),
-            pltpu.VMEM((2, 2, 8 * TALL, COLS), F32),
+            pltpu.VMEM((SLOTS, 2, 8 * TALL, COLS), F32),
             pltpu.VMEM((LAT, SLOTS, ROWS, COLS), F32),
-            dma((2, ENS * LAT)), dma((2, ENS * LAT)),
+            dma((2, 2 * DEPTH)), dma((2, 2 * DEPTH)),
+            dma((ENS,)), dma((ENS, LAT)),
             dma((LON,)), dma((LON,)),
             dma((LAT,)), dma((LAT,)),
             dma((LAT,)), dma((LAT,)),
-            dma((2,)),
+            dma((5,)),
             dma((2,)), dma((2,)),
-            dma((2, 2)), dma((2, 2)),
-            dma((2, LAT)), dma((2, LAT)),
+            dma((3, 2)), dma((3, 2)),
+            dma((3, LAT)), dma((3, LAT)),
         ],
         compiler_params=pltpu.CompilerParams(
-            collective_id=0, has_side_effects=True, vmem_limit_bytes=48 * 2**20
+            collective_id=0, has_side_effects=True, vmem_limit_bytes=60 * 2**20
         ),
-    )(members, grad, index, lat_taps, lon_taps, order, pack, spread)
-
-
-def selections():
-    to, frm = jnp.arange(256)[:, None], jnp.arange(256)[None, :]
-    q, j, g, ch = to // 64, to // 16 % 4, to // 4 % 4, to % 4
-    order = (frm == (4 * g + j) * 16 + 4 * q + ch).astype(BF16)
-    row, col = jnp.arange(1024)[:, None], jnp.arange(256)[None, :]
-    side, j, cc = col // COLS, col % COLS // REACH, col % REACH
-    edge = jnp.where(side == 0, cc, COLS - REACH + cc)
-    pack = (row == j * COLS + edge).astype(BF16)
-    spread = (jnp.arange(COLS)[:, None] == edge).astype(BF16)
-    return order, pack, spread
+    )(members, grad, index, lat_taps, lon_taps)
 
 
 def local(grad_tokens, token_index, members, lat_taps, lon_taps):
-    order, pack, spread = selections()
-    total = increments(members, grad_tokens, token_index, lat_taps, lon_taps, order, pack, spread)
+    total = increments(members, grad_tokens, token_index, lat_taps, lon_taps)
     return total / (2 * ENS - 1)
 
 

time: 91.9 us -> 79.2 us (0.86)
  Pallas kernels: 88.8 us -> 77.5 us
  local copies, waits for them, and re-layouts: 1.76 us -> 0 us
    pallas_call x1, Pallas kernels: 88.8 us -> 77.5 us  [increments(): pl.pallas_call(kernel, out_shape=jax.ShapeDtypeStruct((GROUP, ROWS, COLS)...]
    unnamed x10 -> x0, local copies, waits for them, and re-layouts: 1.76 us -> none
where the time goes in v3:
time: 79.2 us; the launch traced here: 79.1 us
  Pallas kernels  77.5 us (98%)
  other arithmetic  1.55 us (2%)
    pallas_call x1, Pallas kernels, increments(): pl.pallas_call(kernel, out_shape=jax.ShapeDtypeStruct((GROUP, ROWS, COLS)...  77.5 us

profile of v3, /device:TPU:1, one launch (start us, length us, event | category | flops | bytes accessed | tf_op | source)
XLA Modules:
  0.0 79.1 jit_solution(11739728608231916903)
XLA Ops:
  0.0 77.5 %shard_map.55 = f32[13,16,128]{2,1,0:T(8,128)} custom-call(bf16[2,104,16,128]{3,2,1,0:T(8,128)(2,1)} %members.1, bf16[104,2048]{1,0:T(8,128)(2,1)} %grad.1, s32[16,128]{1,0:T(8,128)} %index.1, f32[17]{0:T(128)} %lat_taps.1, f32[17]{0:T(128)} %lon_taps.1), custom_call_target="tpu_custom_call" | custom-call | tf_op jit(solution)/shard_map/pallas_call | solution.py:428
  77.5 1.5 %broadcast_multiply_fusion = f32[13,16,128]{2,1,0:T(8,128)} fusion(f32[13,16,128]{2,1,0:T(8,128)} %shard_map.55), kind=kLoop, calls=%fused_computation | loop fusion | flops 26624 | bytes 212992 | tf_op jit(solution)/shard_map/div | solution.py:476

commit v4 on v3

--- a/solution.py
+++ b/solution.py
@@ -244,12 +244,8 @@
     def tokens_here(q):
         remote(sorted_t.at[q], moved_t.at[q], u_send.at[q], u_recv.at[q], (e, q, n)).wait_recv()
         remote(moved_i.at[q], moved_i.at[q], i_send.at[q], i_recv.at[q], (e, q, n)).wait_recv()
-        sorted_copy(q).wait_send()
-        index_copy(q).wait_send()
 
     others(tokens_here)
-    for dn in range(1, LON):
-        token_copy(dn).wait_send()
 
     parts = [moved_t[:, 16 * j : 16 * j + 16, :].astype(F32).reshape(64, COLS) for j in range(4)]
     lane = iota((64, COLS), 1) // PIECE
@@ -408,11 +404,15 @@
         complete(2, (SPARE,))
 
     middle((3,))
+    complete(1, (3,))
     for p in range(2):
         for d, kk in pairs:
             member_copy(p, d, kk).wait_send()
     for_spares(lambda de: spare_copy(de).wait_send())
-    complete(1, (3,))
+    for dn in range(1, LON):
+        token_copy(dn).wait_send()
+    others(lambda q: sorted_copy(q).wait_send())
+    others(lambda q: index_copy(q).wait_send())
     for p in range(2):
         others(lambda q, p=p: result_here(p, q).wait_recv())
         others(lambda q, p=p: result_copy(p, q).wait_send())

time: 79.2 us -> 79.2 us (level)
  no operation moved by 1% of the time
where the time goes in v4:
time: 79.2 us; the launch traced here: 79.1 us
  Pallas kernels  77.5 us (98%)
  other arithmetic  1.55 us (2%)
    pallas_call x1, Pallas kernels, increments(): pl.pallas_call(kernel, out_shape=jax.ShapeDtypeStruct((GROUP, ROWS, COLS)...  77.5 us

profile of v4, /device:TPU:1, one launch (start us, length us, event | category | flops | bytes accessed | tf_op | source)
XLA Modules:
  0.0 79.1 jit_solution(3056015119933376402)
XLA Ops:
  0.0 77.5 %shard_map.55 = f32[13,16,128]{2,1,0:T(8,128)} custom-call(bf16[2,104,16,128]{3,2,1,0:T(8,128)(2,1)} %members.1, bf16[104,2048]{1,0:T(8,128)(2,1)} %grad.1, s32[16,128]{1,0:T(8,128)} %index.1, f32[17]{0:T(128)} %lat_taps.1, f32[17]{0:T(128)} %lon_taps.1), custom_call_target="tpu_custom_call" | custom-call | tf_op jit(solution)/shard_map/pallas_call | solution.py:428
  77.5 1.5 %broadcast_multiply_fusion = f32[13,16,128]{2,1,0:T(8,128)} fusion(f32[13,16,128]{2,1,0:T(8,128)} %shard_map.55), kind=kLoop, calls=%fused_computation | loop fusion | flops 26624 | bytes 212992 | tf_op jit(solution)/shard_map/div | solution.py:476
